TPU v7x, 256 devices: a whole 4x4x8 slice. The times are simulated.
256 devices in a mesh: section: 2 (over x_hi), expert: 128 (over z, y, x_lo, core).
Axes of the slice: x: 4 (x_hi: 2, x_lo: 2; x = x_hi * 2 + x_lo), y: 4, z: 8, core: 2. Of those that a mesh axis runs over, the one named last changes fastest.
Arguments:
- tokens: bfloat16 [16384, 2048], P('expert'), may hold values from -6 to 6
- memory: bfloat16 [256, 32, 2, 2048], P('expert', 'section'), may hold values from -51 to 51
- target_len: int32 [256], P('expert'), may hold values from 32 to 64
- source_len: int32 [256], P('expert'), may hold values from 8 to 32
- attn_gain: float32 [2048], replicated, may hold values from 0.5 to 1.5
- w_query: bfloat16 [2048, 2048], P('expert', 'section'), may hold values from -0.125 to 0.125
- w_out: bfloat16 [2048, 2048], P('section', 'expert'), may hold values from -0.125 to 0.125
- moe_gain: float32 [2048], replicated, may hold values from 0.5 to 1.5
- w_router: bfloat16 [2048, 64], replicated, may hold values from -0.125 to 0.125
- expert_ids: int32 [16384, 2], P('expert'), may hold values from 0 to 63, all different within a row; in each aligned block of 128 rows (0 to 127, 128 to 255, ...) at most 6 rows name the same one
- w_up: bfloat16 [128, 2048, 2048], P('expert', None, 'section'), may hold values from -0.125 to 0.125
- w_down: bfloat16 [128, 2048, 2048], P('expert', 'section'), may hold values from -0.09375 to 0.09375
Outputs:
- layer_out: bfloat16 [16384, 2048], P('expert')
Inputs may be any that keep to these rules, and one draw needn't show every extreme that they name: `expert_ids`: within the 128 tokens of one index of the expert axis, no expert is named by more than 6 tokens, a bound that some block reaches; the two experts of a token differ.
All inputs are finite; a program needn't handle non-finite values.
Results may differ from a plain program's by a relative error of at most 0.015.
Values may be sent and summed in bfloat16 or wider, within the bound.
A program may use at most 64 MiB of HBM per device.

v0:
```python
import jax
import jax.numpy as jnp
from jax import lax
from jax.sharding import PartitionSpec as P

HD = 128


def layer_norm(values, gain):
    center = values - jnp.mean(values, axis=-1, keepdims=True)
    spread = jnp.mean(center * center, axis=-1, keepdims=True)
    return center * lax.rsqrt(spread + 1e-05) * gain


def assign_slots(expert_ids, live_rows, experts, capacity):
    flat_ids = expert_ids.reshape(-1)
    alive_rows = jnp.repeat(live_rows, 2)
    onehot = (
        (flat_ids[:, None] == jnp.arange(experts, dtype=jnp.int32)[None, :]) & alive_rows[:, None]
    ).astype(jnp.int32)
    before = jnp.cumsum(onehot, axis=0) - onehot
    slot_index = jnp.sum(before * onehot, axis=1)
    target = jnp.where(alive_rows, flat_ids * capacity + slot_index, -1)
    return target.reshape(expert_ids.shape)


def expert_part(arrived, up_block, down_block):
    width = arrived.shape[-1]
    rows = arrived.reshape(-1, width)
    hidden = jnp.maximum(jnp.dot(rows, up_block, preferred_element_type=jnp.float32), 0.0).astype(
        jnp.bfloat16
    )
    part_out = jnp.dot(hidden, down_block, preferred_element_type=jnp.float32).astype(jnp.bfloat16)
    return part_out.reshape(arrived.shape)


def body(
    tokens,
    memory,
    target_len,
    source_len,
    attn_gain,
    w_query,
    w_out,
    moe_gain,
    w_router,
    expert_ids,
    w_up,
    w_down,
):
    token_count, width = tokens.shape
    seq_count = target_len.shape[0]
    target_span = token_count // seq_count
    experts = w_router.shape[1]
    capacity = 2 * (3 * token_count // (2 * experts))
    residual_in = tokens.astype(jnp.float32)
    normed = layer_norm(residual_in, attn_gain).astype(jnp.bfloat16)
    query = jnp.dot(
        normed,
        lax.all_gather(w_query, "expert", axis=0, tiled=True),
        preferred_element_type=jnp.float32,
    ).astype(jnp.bfloat16)
    arrived_memory = lax.all_to_all(memory, "section", split_axis=3, concat_axis=1, tiled=True)
    source_span = arrived_memory.shape[1]
    head_count = w_query.shape[1] // HD
    query_heads = query.reshape(seq_count, target_span, head_count, HD)
    key_heads = arrived_memory[:, :, 0].reshape(seq_count, source_span, head_count, HD)
    value_heads = arrived_memory[:, :, 1].reshape(seq_count, source_span, head_count, HD)
    scores = jnp.einsum(
        "sqhd,skhd->shqk", query_heads, key_heads, preferred_element_type=jnp.float32
    ) * HD ** (-0.5)
    visible = jnp.arange(source_span, dtype=jnp.int32)[None, :] < source_len[:, None]
    scores = jnp.where(visible[:, None, None, :], scores, -1e30)
    weights = jax.nn.softmax(scores, axis=-1).astype(jnp.bfloat16)
    context = jnp.einsum(
        "shqk,skhd->sqhd", weights, value_heads, preferred_element_type=jnp.float32
    ).astype(jnp.bfloat16)
    context = context.reshape(token_count, head_count * HD)
    head_part = jnp.dot(
        context,
        lax.all_gather(w_out, "expert", axis=1, tiled=True),
        preferred_element_type=jnp.float32,
    )
    after_attn = residual_in + lax.psum(head_part.astype(jnp.bfloat16), "section").astype(
        jnp.float32
    )
    moe_in = layer_norm(after_attn, moe_gain).astype(jnp.bfloat16)
    logits = jnp.dot(moe_in, w_router, preferred_element_type=jnp.float32)
    picked = jnp.take_along_axis(logits, expert_ids, axis=1)
    gates = jax.nn.sigmoid(picked - picked[:, ::-1])
    live_rows = (jnp.arange(target_span, dtype=jnp.int32)[None, :] < target_len[:, None]).reshape(
        -1
    )
    targets = assign_slots(expert_ids, live_rows, experts, capacity)
    slot_range = jnp.arange(experts * capacity, dtype=jnp.int32)
    send_table = jnp.any(targets[:, :, None] == slot_range[None, None, :], axis=1).astype(
        jnp.bfloat16
    )
    buffer = lax.dot_general(
        send_table, moe_in, (((0,), (0,)), ((), ())), preferred_element_type=jnp.float32
    ).astype(jnp.bfloat16)
    up_block = w_up[0]
    down_block = w_down[0]
    outgoing = jnp.repeat(buffer.reshape(experts, capacity, width), 2, axis=0)
    part_out = expert_part(
        lax.all_to_all(outgoing, "expert", split_axis=0, concat_axis=0, tiled=True),
        up_block,
        down_block,
    )
    returned = lax.all_to_all(part_out, "expert", split_axis=0, concat_axis=0, tiled=True)
    pair_total = jnp.sum(returned.reshape(experts, 2, capacity, width).astype(jnp.float32), axis=1)
    half_out = lax.optimization_barrier(pair_total.astype(jnp.bfloat16))
    combined = half_out.astype(jnp.float32)
    combined = combined.reshape(experts * capacity, width)
    safe_targets = jnp.where(targets < 0, 0, targets)
    picks = combined[safe_targets]
    gate_weight = jnp.where(targets < 0, 0.0, gates)
    moe_part = jnp.sum(picks * gate_weight[:, :, None], axis=1)
    moe_total = lax.psum(moe_part.astype(jnp.bfloat16), "section").astype(jnp.float32)
    return (after_attn + moe_total).astype(jnp.bfloat16)


def solution(mesh):
    return jax.shard_map(
        body,
        mesh=mesh,
        in_specs=(
            P("expert", None),
            P("expert", "section", None, None),
            P("expert"),
            P("expert"),
            P(),
            P("expert", "section"),
            P("section", "expert"),
            P(),
            P(),
            P("expert", None),
            P("expert", None, "section"),
            P("expert", "section", None),
        ),
        out_specs=P("expert", None),
        check_vma=False,
    )
```

profile of v0, /device:TPU:1, one launch (start us, length us, event | category | flops | bytes accessed | tf_op | source)
XLA Modules:
  0.0 792.9 jit_solution(6130838812788815426)
XLA Ops:
  6.5 0.7 all-gather.3.cloned.1.call-update
  8.0 4.3 copy.98
  12.3 2.8 reshape.162
  15.1 4.8 all-to-all-start
  20.6 5.0 all-to-all-done
  25.5 1.4 reshape.163
  26.9 2.6 copy.100
  29.6 198.8 %all-gather.3.cloned.1.call-done = bf16[2048,1024]{1,0:T(8,128)(2,1)} async-done(((bf16[16,1024]{1,0:T(8,128)(2,1)}), bf16[2048,1024]{1,0:T(8,128)(2,1)}) %all-gather.3.cloned.1.call-update) | async-done | bytes 4194320 | tf_op jit(solution)/shard_map/all_gather | solution.py:60
  228.4 3.0 fusion.13
  232.2 212.1 %all-gather.5.cloned.1.call-done = bf16[1024,2048]{0,1:T(8,128)(2,1)} async-done(((bf16[1024,16]{0,1:T(8,128)(2,1)}), bf16[1024,2048]{0,1:T(8,128)(2,1)}) %all-gather.5.cloned.1.call-update) | async-done | bytes 4194320 | tf_op jit(solution)/shard_map/all_gather | solution.py:81
  444.4 4.5 convolution_convert_fusion.1
  451.4 38.5 %all-reduce.3.cloned.1.call-done = bf16[128,2048]{1,0:T(8,128)(2,1)} async-done(((bf16[128,2048]{1,0:T(8,128)(2,1)}), bf16[128,2048]{1,0:T(8,128)(2,1)}) %all-reduce.3.cloned.1.call-update) | async-done | bytes 524304 | tf_op jit(solution)/shard_map/psum | solution.py:84
  489.9 1.3 fusion.20
  491.1 1.3 multiply_reduce_fusion.1
  492.5 1.3 multiply_convert_fusion
  494.1 2.0 gather_fusion.1
  496.5 1.8 convolution_convert_fusion
  498.3 2.5 reshape.130
  501.3 106.0 %all_to_all.28 = bf16[128,6,2048]{2,1,0:T(8,128)(2,1)} all-to-all(bf16[128,6,2048]{2,1,0:T(8,128)(2,1)S(1)} %bitcast.76), channel_id=1, replica_groups=mesh['section'=2,'expert'=128] {'expert'}, dimensions={0} | all-to-all | bytes 6291456 | tf_op jit(solution)/shard_map/all_to_all | solution.py:106
  607.3 4.9 reshape.132
  612.2 5.7 maximum_convert_fusion
  618.0 3.6 fusion.5
  621.6 2.9 reshape.133
  624.5 9.3 %all-to-all-start.2 = ((bf16[128,6,2048]{2,1,0:T(8,128)(2,1)}), bf16[128,6,2048]{2,1,0:T(8,128)(2,1)}, u32[]{:S(2)}, u32[]{:S(2)}) async-start(bf16[128,6,2048]{2,1,0:T(8,128)(2,1)} %reshape.133), calls=%async_computation.2 | async-start | bytes 8388608 | tf_op jit(solution)/shard_map/all_to_all | solution.py:110
  634.4 93.6 %all-to-all-done.2 = bf16[128,6,2048]{2,1,0:T(8,128)(2,1)} async-done(((bf16[128,6,2048]{2,1,0:T(8,128)(2,1)}), bf16[128,6,2048]{2,1,0:T(8,128)(2,1)}, u32[]{:S(2)}, u32[]{:S(2)}) %all-to-all-start.2) | async-done | bytes 3145760 | tf_op jit(solution)/shard_map/all_to_all | solution.py:110
  728.1 5.2 bitcast_reduce_fusion
  733.2 2.5 reshape.139
  735.8 2.7 gather_fusion
  738.5 2.6 reshape.141
  741.1 3.9 multiply_reduce_fusion
  745.0 39.3 %all-reduce.5.cloned.1.call-done = bf16[128,2048]{1,0:T(8,128)(2,1)} async-done(((bf16[128,2048]{1,0:T(8,128)(2,1)}), bf16[128,2048]{1,0:T(8,128)(2,1)}) %all-reduce.5.cloned.1.call-update) | async-done | bytes 524304 | tf_op jit(solution)/shard_map/psum | solution.py:119
  784.3 2.1 add_convert_fusion
  (75 shorter events, 6.5 us)
Async XLA Ops:
  6.5 487.3 %copy-start = (bf16[2048,64]{0,1:T(8,128)(2,1)S(1)}, bf16[2048,64]{0,1:T(8,128)(2,1)}, u32[]{:S(2)}) copy-start(bf16[2048,64]{0,1:T(8,128)(2,1)} %param.20) | copy-start | bytes 786436
  6.5 13.4 %copy-start.1 = (bf16[128,2048]{1,0:T(8,128)(2,1)S(1)}, bf16[128,2048]{1,0:T(8,128)(2,1)}, u32[]{:S(2)}) copy-start(bf16[128,2048]{1,0:T(8,128)(2,1)} %param.12) | copy-start | bytes 1572868
  6.5 221.8 %all-gather.3.cloned.1.call-start = ((), (), s32[]{:S(2)}) async-start(), calls=%async_computation.3 | async-start | bytes 4227072 | tf_op jit(solution)/shard_map/all_gather | solution.py:60
  7.3 437.1 %all-gather.5.cloned.1.call-start = ((), (), s32[]{:S(2)}) async-start(), calls=%async_computation.4 | async-start | bytes 4227072 | tf_op jit(solution)/shard_map/all_gather | solution.py:81
  8.0 12.4 %copy-start.4 = (s32[128,2]{0,1:T(2,128)S(1)}, s32[128,2]{0,1:T(2,128)}, u32[]{:S(2)}) copy-start(s32[128,2]{0,1:T(2,128)} %param.21) | copy-start | bytes 3076
  8.0 12.5 %copy-start.8 = (s32[2]{0:T(128)S(1)}, s32[2]{0:T(128)}, u32[]{:S(2)}) copy-start(s32[2]{0:T(128)} %param.15) | copy-start | bytes 28
  15.1 10.4 %all-to-all-start = ((bf16[2,2,32768]{2,1,0:T(2,128)(2,1)}), bf16[2,2,32768]{2,1,0:T(2,128)(2,1)S(1)}, u32[]{:S(2)}, u32[]{:S(2)}) async-start(bf16[2,2,32768]{2,1,0:T(2,128)(2,1)} %reshape.162), calls=%async_computation | async-start | bytes 524288 | tf_op jit(solution)/shard_map/all_to_all | solution.py:63
  20.0 469.9 %all-reduce.3.cloned.1.call-start = ((), (), s32[]{:S(2)}) async-start(), calls=%async_computation.5 | async-start | bytes 1048576 | tf_op jit(solution)/shard_map/psum | solution.py:84
  20.1 208.2 %copy-start.7 = (f32[2048]{0:T(1024)S(1)}, f32[2048]{0:T(1024)}, u32[]{:S(2)}) copy-start(f32[2048]{0:T(1024)} %param.16) | copy-start | bytes 24580
  232.0 216.9 %copy-start.9 = (s32[2]{0:T(128)S(1)}, s32[2]{0:T(128)}, u32[]{:S(2)}) copy-start(s32[2]{0:T(128)} %param.14) | copy-start | bytes 28
  444.4 48.1 %copy-start.5 = (f32[2048]{0:T(1024)S(1)}, f32[2048]{0:T(1024)}, u32[]{:S(2)}) copy-start(f32[2048]{0:T(1024)} %param.19) | copy-start | bytes 24580
  612.2 5.8 copy-start.6
  624.5 103.6 %all-to-all-start.2 = ((bf16[128,6,2048]{2,1,0:T(8,128)(2,1)}), bf16[128,6,2048]{2,1,0:T(8,128)(2,1)}, u32[]{:S(2)}, u32[]{:S(2)}) async-start(bf16[128,6,2048]{2,1,0:T(8,128)(2,1)} %reshape.133), calls=%async_computation.2 | async-start | bytes 8388608 | tf_op jit(solution)/shard_map/all_to_all | solution.py:110
  633.8 150.5 %all-reduce.5.cloned.1.call-start = ((), (), s32[]{:S(2)}) async-start(), calls=%async_computation.6 | async-start | bytes 1048576 | tf_op jit(solution)/shard_map/psum | solution.py:119
  738.5 45.8 %copy-start.2 = (bf16[128,2048]{1,0:T(8,128)(2,1)S(1)}, bf16[128,2048]{1,0:T(8,128)(2,1)}, u32[]{:S(2)}) copy-start(bf16[128,2048]{1,0:T(8,128)(2,1)} %param.12) | copy-start | bytes 1572868
  738.5 45.8 %copy-start.3 = (bf16[128,2048]{1,0:T(8,128)(2,1)S(1)}, bf16[128,2048]{1,0:T(8,128)(2,1)}, u32[]{:S(2)}) copy-start(bf16[128,2048]{1,0:T(8,128)(2,1)} %all-reduce.3.cloned.1.call-done) | copy-start | bytes 1572868
Sparse Core Ops, SparseCore 0:
  9.2 219.1 all-gather.2
  230.2 214.0 all-gather.4
  449.0 40.7 all-reduce.2
  745.1 39.1 all-reduce.4
where the time goes:
time: 794 us; the launch traced here: 793 us
  waiting for transfers between devices  589 us (74%)
  blocking collectives  106 us (13%)
  local copies, waits for them, and re-layouts  34.1 us (4%)
  matrix products  19.4 us (2%)
  other arithmetic  16.7 us (2%)
  starting transfers between devices  14.4 us (2%)
  between operations  13.5 us (2%)
    all_gather x1, waiting for transfers between devices, body(): lax.all_gather(w_out, 'expert', axis=1, tiled=True)  212 us
    all_gather x1, waiting for transfers between devices, body(): lax.all_gather(w_query, 'expert', axis=0, tiled=True)  199 us
    all_to_all x1, blocking collectives, body(): lax.all_to_all(outgoing, 'expert', split_axis=0, concat_axis=0, tiled=True)  106 us
    all_to_all x1, waiting for transfers between devices, body(): lax.all_to_all(part_out, 'expert', split_axis=0, concat_axis=0, tiled=True)  93.6 us
    psum x1, waiting for transfers between devices, body(): lax.psum(moe_part.astype(jnp.bfloat16), 'section').astype(jnp.float32)  39.3 us
    psum x1, waiting for transfers between devices, body(): lax.psum(head_part.astype(jnp.bfloat16), 'section').astype(jnp.float32)  38.5 us
  transfers between devices with their start and end apart: 6, of which 6 were waited for; matrix products, arithmetic and copies ran while one was open for 2% of the time, Pallas kernels for 0%

commit v1 on v0

v1 whole, which is shorter than its diff:
```python
import functools

import jax
import jax.numpy as jnp
import numpy as np
from jax import lax
from jax.experimental import pallas as pl
from jax.experimental.pallas import tpu as pltpu
from jax.sharding import PartitionSpec as P

MESH = pl.DeviceIdType.MESH
F32 = jnp.float32
BF16 = jnp.bfloat16

HD = 128
D = 2048
HALF = 1024
TOK = 128
CAP = 6
EXPERTS = 64
SLOTS = EXPERTS * CAP
BLOCK = 8 * CAP
CHUNKS = 2
CW = HALF // CHUNKS
NZ, NY, NX = 8, 4, 2


def coords():
    s = lax.axis_index("section")
    e = lax.axis_index("expert")
    return s, e // 16, (e // 4) % 4, (e // 2) % 2, e % 2


def device(s, z, y, x, c):
    return (s, ((z * NY + y) * NX + x) * 2 + c)


class Net:
    def __init__(self, send_sem, recv_sem):
        self.send_sem, self.recv_sem = send_sem, recv_sem
        self.copies = []

    def send(self, src, dst, target):
        k = len(self.copies)
        copy = pltpu.make_async_remote_copy(
            src_ref=src,
            dst_ref=dst,
            send_sem=self.send_sem.at[k],
            recv_sem=self.recv_sem.at[k],
            device_id=target,
            device_id_type=MESH,
        )
        copy.start()
        self.copies.append(copy)
        return copy

    def finish(self):
        for copy in self.copies:
            copy.wait_send()


def recv(copies):
    for copy in copies:
        copy.wait_recv()


def gather_z_last(net, buf, cols, forwards):
    s, z, y, x, c = coords()
    view = lambda *idx: buf.at[(*idx, slice(None), cols)]
    sibling = device(s, z, y, x, 1 - c)
    mine = view(z, y * 2 + x, c)
    a = net.send(mine, mine, device(s, z, y, 1 - x, c))
    yield
    recv([a])
    pair = view(z, pl.ds(y * 2, 2), c)
    b = [net.send(pair, pair, device(s, z, (y + d) % NY, x, c)) for d in (1, 3, 2)]
    yield
    recv(b)
    slab = view(z, slice(None), c)
    up, down = device(s, (z + 1) % NZ, y, x, c), device(s, (z + 7) % NZ, y, x, c)
    u, d = net.send(slab, slab, up), net.send(slab, slab, down)
    forwards.append(net.send(slab, slab, sibling))
    for step in range(1, 4):
        yield
        recv([u])
        block = view((z + 8 - step) % NZ, slice(None), c)
        part = block if step < 3 else view((z + 8 - step) % NZ, pl.ds(0, 4), c)
        u = net.send(part, part, up)
        forwards.append(net.send(block, block, sibling))
        recv([d])
        block = view((z + step) % NZ, slice(None), c)
        part = block if step < 3 else view((z + step) % NZ, pl.ds(4, 4), c)
        d = net.send(part, part, down)
        forwards.append(net.send(block, block, sibling))
    yield
    recv([u, d])
    block = view((z + 4) % NZ, slice(None), c)
    forwards.append(net.send(block, block, sibling))


def gather_y_last(net, buf, cols, forwards):
    s, z, y, x, c = coords()
    view = lambda *idx: buf.at[(*idx, slice(None), cols)]
    sibling = device(s, z, y, x, 1 - c)
    mine = view(z, y * 2 + x, c)
    a = [net.send(mine, mine, device(s, (z + d) % NZ, y, x, c)) for d in (1, 7, 2, 6, 3, 5, 4)]
    yield
    recv(a)
    line = view(slice(None), y * 2 + x, c)
    b = net.send(line, line, device(s, z, y, 1 - x, c))
    yield
    recv([b])
    up, down = device(s, z, (y + 1) % NY, x, c), device(s, z, (y + 3) % NY, x, c)
    slab = view(slice(None), pl.ds(y * 2, 2), c)
    u, d = net.send(slab, slab, up), net.send(slab, slab, down)
    forwards.append(net.send(slab, slab, sibling))
    yield
    recv([u])
    below = ((y + 3) % NY) * 2
    part = view(pl.ds(0, 4), pl.ds(below, 2), c)
    u = net.send(part, part, up)
    block = view(slice(None), pl.ds(below, 2), c)
    forwards.append(net.send(block, block, sibling))
    recv([d])
    above = ((y + 1) % NY) * 2
    part = view(pl.ds(4, 4), pl.ds(above, 2), c)
    d = net.send(part, part, down)
    block = view(slice(None), pl.ds(above, 2), c)
    forwards.append(net.send(block, block, sibling))
    yield
    recv([u, d])
    block = view(slice(None), pl.ds(((y + 2) % NY) * 2, 2), c)
    forwards.append(net.send(block, block, sibling))


def iota(shape, dim):
    return lax.broadcasted_iota(jnp.int32, shape, dim)


def nt_dot(a, b):
    return lax.dot_general(a, b, (((1,), (1,)), ((), ())), preferred_element_type=F32)


def dot(a, b):
    return jnp.dot(a, b, preferred_element_type=F32)


def kernel(
    tokens_ref,
    memory_ref,
    target_len_ref,
    source_len_ref,
    attn_gain_ref,
    w_query_ref,
    w_out_ref,
    moe_gain_ref,
    w_router_ref,
    ids_ref,
    ids_t_ref,
    perm_ref,
    perm_kv_ref,
    w_up_hbm,
    w_down_hbm,
    out_ref,
    wq,
    wo,
    w_up,
    w_down,
    mem,
    kv,
    normed,
    query_acc,
    context,
    head_send,
    head_recv,
    after,
    stat_send,
    stat_recv,
    logit_send,
    logit_recv,
    table,
    z_send,
    z_recv,
    p_send,
    rows,
    acc,
    hidden,
    part_send,
    part_recv,
    part_own,
    sec_send,
    sec_recv,
    rp_send,
    rp_recv,
    rz_send,
    rz_recv,
    out_send,
    out_recv,
    send_sem,
    recv_sem,
    load_sem,
):
    s, z, y, x, c = coords()
    chip = y * 2 + x
    sibling, partner = device(s, z, y, x, 1 - c), device(1 - s, z, y, x, c)
    z_peers = [device(s, (z + d) % NZ, y, x, c) for d in (4, 3, 5, 2, 6, 1, 7)]
    plane = [(1, 1), (3, 1), (2, 1), (2, 0), (0, 1), (1, 0), (3, 0)]
    p_peers = [device(s, z, (y + dy) % NY, (x + dx) % NX, c) for dy, dx in plane]
    p_chips = [((y + dy) % NY) * 2 + (x + dx) % NX for dy, dx in plane]

    load_up = pltpu.make_async_copy(w_up_hbm, w_up, load_sem.at[0])
    load_down = pltpu.make_async_copy(w_down_hbm, w_down, load_sem.at[1])
    load_up.start()
    load_down.start()

    barrier = pltpu.get_barrier_semaphore()
    peers = [sibling, partner, *z_peers, *p_peers]
    for peer in peers:
        pl.semaphore_signal(barrier, inc=1, device_id=peer, device_id_type=MESH)
    wq[z, chip, c] = w_query_ref[...]
    wo[z, chip, c] = w_out_ref[...]
    pl.semaphore_wait(barrier, len(peers))

    net = Net(send_sem, recv_sem)
    col0 = pl.multiple_of(s * HALF, HALF)
    col1 = pl.multiple_of((1 - s) * HALF, HALF)
    full = pl.ds(0, HALF)
    q_forwards, o_forwards = [], []
    gather_q = gather_z_last(net, wq, full, q_forwards)
    gather_o = gather_y_last(net, wo, full, o_forwards)
    next(gather_q)
    next(gather_o)
    mem_copy = net.send(memory_ref.at[:, pl.ds(col1, HALF)], mem.at[s], partner)
    mem[s] = memory_ref[:, pl.ds(col0, HALF)]

    next(gather_q)

    values = tokens_ref[...].astype(F32)
    center = values - jnp.mean(values, axis=-1, keepdims=True)
    spread = jnp.mean(center * center, axis=-1, keepdims=True)
    normed[...] = (center * lax.rsqrt(spread + 1e-05) * attn_gain_ref[...]).astype(BF16)

    next(gather_o)
    next(gather_q)

    tl0, tl1 = target_len_ref[0], target_len_ref[1]
    t = iota((1, TOK), 1)
    live = t < jnp.where(t < 64, tl0, tl1 + 64)
    i0, i1 = ids_t_ref[0:1, :], ids_t_ref[1:2, :]
    experts = iota((EXPERTS, TOK), 0)
    hit0, hit1 = (experts == i0) & live, (experts == i1) & live
    earlier = (iota((TOK, TOK), 0) < iota((TOK, TOK), 1)).astype(F32).astype(BF16)
    before = dot((hit0.astype(F32) + hit1.astype(F32)).astype(BF16), earlier)
    slot0 = jnp.sum(jnp.where(hit0, before, 0.0), axis=0, keepdims=True)
    slot1 = jnp.sum(jnp.where(hit1, before, 0.0), axis=0, keepdims=True)
    to0 = jnp.where(live, i0.astype(F32) * CAP + slot0, -1.0)
    to1 = jnp.where(live, i1.astype(F32) * CAP + slot1, -1.0)
    places = iota((SLOTS, TOK), 0).astype(F32)
    table[...] = ((places == to0) | (places == to1)).astype(F32).astype(BF16)

    t = iota((TOK, 1), 0)
    live = t < jnp.where(t < 64, tl0, tl1 + 64)
    i0, i1 = ids_ref[:, 0:1], ids_ref[:, 1:2]
    experts = iota((TOK, EXPERTS), 1)
    pick0, pick1 = experts == i0, experts == i1
    hit0, hit1 = pick0 & live, pick1 & live
    earlier = (iota((TOK, TOK), 1) < iota((TOK, TOK), 0)).astype(F32).astype(BF16)
    before = dot(earlier, (hit0.astype(F32) + hit1.astype(F32)).astype(BF16))
    slot0 = jnp.sum(jnp.where(hit0, before, 0.0), axis=1, keepdims=True)
    slot1 = jnp.sum(jnp.where(hit1, before, 0.0), axis=1, keepdims=True)
    from0 = jnp.where(live, i0.astype(F32) * CAP + slot0, -1.0)
    from1 = jnp.where(live, i1.astype(F32) * CAP + slot1, -1.0)

    next(gather_o)
    next(gather_q)
    recv([mem_copy])
    kv[...] = dot(perm_kv_ref[...], mem[...].reshape(TOK, HALF)).astype(BF16)
    next(gather_q)
    next(gather_o)
    next(gather_q)
    for _ in gather_o:
        pass
    for _ in gather_q:
        pass
    recv(q_forwards)

    query_acc[...] = jnp.zeros_like(query_acc)

    @pl.loop(0, NZ)
    def _(k):
        columns = pl.ds(pl.multiple_of(k * 256, 256), 256)
        query_acc[...] += dot(normed[:, columns], wq[k].reshape(256, HALF))

    sl0, sl1 = source_len_ref[0], source_len_ref[1]
    q_row, k_col = iota((TOK, 64), 0), iota((TOK, 64), 1)
    visible = (k_col >= jnp.where(q_row < 64, 0, 32)) & (
        k_col < jnp.where(q_row < 64, sl0, sl1 + 32)
    )
    for h in range(HALF // HD):
        head = slice(h * HD, (h + 1) * HD)
        query = query_acc[:, head].astype(BF16)
        scores = nt_dot(query, kv[0:64, head]) * HD ** (-0.5)
        scores = jnp.where(visible, scores, -1e30)
        scores = jnp.exp(scores - jnp.max(scores, axis=-1, keepdims=True))
        weights = (scores / jnp.sum(scores, axis=-1, keepdims=True)).astype(BF16)
        context[:, head] = dot(weights, kv[64:128, head]).astype(BF16)

    recv(o_forwards)
    for ch in range(CHUNKS):
        other = wo[pl.ds((1 - s) * 4 + 2 * ch, 2)].reshape(CW, HALF)
        head_send[ch] = nt_dot(context[...], other).astype(BF16)
        copy = net.send(head_send.at[ch], head_recv.at[ch], partner)
        head_copies = [copy] if ch == 0 else head_copies + [copy]
    for ch in range(CHUNKS):
        own = wo[pl.ds(s * 4 + 2 * ch, 2)].reshape(CW, HALF)
        columns = pl.ds(pl.multiple_of(s * HALF + ch * CW, CW), CW)
        after[:, ch * CW : (ch + 1) * CW] = tokens_ref[:, columns].astype(F32) + nt_dot(context[...], own)
    for ch in range(CHUNKS):
        recv([head_copies[ch]])
        after[:, ch * CW : (ch + 1) * CW] += head_recv[ch].astype(F32)

    values = after[...]
    mean = jnp.mean(values, axis=-1, keepdims=True)
    center = values - mean
    square = jnp.sum(center * center, axis=-1, keepdims=True)
    stat_send[...] = jnp.where(iota((TOK, 128), 1) < 64, mean, square)
    stat_copy = net.send(stat_send, stat_recv, partner)
    recv([stat_copy])
    mean_other, square_other = stat_recv[:, 0:1], stat_recv[:, 64:65]
    gap = mean - mean_other
    spread = (square + square_other + gap * gap * (HALF / 2)) * (1.0 / D)
    mean = (mean + mean_other) * 0.5
    moe_in = (
        (values - mean) * lax.rsqrt(spread + 1e-05) * moe_gain_ref[:, pl.ds(col0, HALF)]
    ).astype(BF16)

    own_z = pl.ds(pl.multiple_of(z * BLOCK, 16), BLOCK)
    z_copies = []
    for ch in range(CHUNKS):
        z_send[ch] = dot(table[...], moe_in[:, ch * CW : (ch + 1) * CW]).astype(BF16)
        copies = []
        for k, d in enumerate((4, 3, 5, 2, 6, 1, 7)):
            there = pl.ds(pl.multiple_of((z + d) % NZ * BLOCK, 16), BLOCK)
            copies.append(net.send(z_send.at[ch, there], z_recv.at[ch, own_z], z_peers[k]))
        z_recv[ch, own_z] = z_send[ch, own_z]
        z_copies.append(copies)

    logit_send[...] = jnp.zeros_like(logit_send)
    logit_send[:, 0:EXPERTS] = dot(moe_in, w_router_ref[pl.ds(col0, HALF), :])
    logit_copy = net.send(logit_send, logit_recv, partner)

    own_chip = pl.ds(pl.multiple_of(chip * BLOCK, 16), BLOCK)
    p_copies = []
    for ch in range(CHUNKS):
        recv(z_copies[ch])
        p_send[ch] = dot(perm_ref[...], z_recv[ch]).astype(BF16)
        copies = []
        for k, there in enumerate(p_chips):
            block = pl.ds(pl.multiple_of(there * BLOCK, 16), BLOCK)
            copies.append(
                net.send(p_send.at[ch, block], rows.at[c, s, ch, own_chip], p_peers[k])
            )
        rows[c, s, ch, own_chip] = p_send[ch, own_chip]
        p_copies.append(copies)

    load_up.wait()

    def add_up(cc, ss, ch, first):
        depth = pl.ds(pl.multiple_of(ss * HALF + ch * CW, CW), CW)

        @pl.loop(0, HALF // 256)
        def _(n):
            tile = pl.ds(pl.multiple_of(n * 256, 256), 256)
            product = dot(rows[cc, ss, ch], w_up[depth, tile])
            if first:
                acc[cc, :, tile] = product
            else:
                acc[cc, :, tile] += product

    s_copies, own_forwards, other_forwards = [], [], []
    for ch in range(CHUNKS):
        recv(p_copies[ch])
        mine = rows.at[c, s, ch]
        s_copies.append(net.send(mine, mine, partner))
        own_forwards.append(net.send(mine, mine, sibling))
        add_up(c, s, ch, ch == 0)
    for ch in range(CHUNKS):
        recv([own_forwards[ch]])
        add_up(1 - c, s, ch, ch == 0)
    for ch in range(CHUNKS):
        recv([s_copies[ch]])
        theirs = rows.at[c, 1 - s, ch]
        other_forwards.append(net.send(theirs, theirs, sibling))
        add_up(c, 1 - s, ch, False)
    hidden[c] = jnp.maximum(acc[c], 0.0).astype(BF16)
    for ch in range(CHUNKS):
        recv([other_forwards[ch]])
        add_up(1 - c, 1 - s, ch, False)
    hidden[1 - c] = jnp.maximum(acc[1 - c], 0.0).astype(BF16)

    load_down.wait()

    def down(cc, q, into):
        half = 1 - s if q < CHUNKS else s
        start = half * HALF + (q % CHUNKS) * CW
        for n in range(CW // 256):
            tile = pl.ds(pl.multiple_of(start + n * 256, 256), 256)
            into[q, :, n * 256 : (n + 1) * 256] = dot(hidden[cc], w_down[:, tile]).astype(BF16)

    part_copies = []
    for q in range(2 * CHUNKS):
        down(1 - c, q, part_send)
        part_copies.append(net.send(part_send.at[q], part_recv.at[q], sibling))
        down(c, q, part_own)
    sec_copies = []
    for q in range(CHUNKS):
        recv([part_copies[q]])
        sec_send[q] = (part_own[q].astype(F32) + part_recv[q].astype(F32)).astype(BF16)
        sec_copies.append(net.send(sec_send.at[q], sec_recv.at[q], partner))

    rp_copies = []
    for ch in range(CHUNKS):
        q = CHUNKS + ch
        recv([part_copies[q]])
        half_out = (part_own[q].astype(F32) + part_recv[q].astype(F32)).astype(BF16)
        recv([sec_copies[ch]])
        rp_send[ch] = (half_out.astype(F32) + sec_recv[ch].astype(F32)).astype(BF16)
        copies = []
        for k, there in enumerate(p_chips):
            block = pl.ds(pl.multiple_of(there * BLOCK, 16), BLOCK)
            copies.append(net.send(rp_send.at[ch, block], rp_recv.at[ch, own_chip], p_peers[k]))
        rp_recv[ch, own_chip] = rp_send[ch, own_chip]
        rp_copies.append(copies)

    rz_copies = []
    for ch in range(CHUNKS):
        recv(rp_copies[ch])
        rz_send[ch] = dot(perm_ref[...], rp_recv[ch]).astype(BF16)
        copies = []
        for k, d in enumerate((4, 3, 5, 2, 6, 1, 7)):
            there = pl.ds(pl.multiple_of((z + d) % NZ * BLOCK, 16), BLOCK)
            copies.append(net.send(rz_send.at[ch, there], rz_recv.at[ch, own_z], z_peers[k]))
        rz_recv[ch, own_z] = rz_send[ch, own_z]
        rz_copies.append(copies)

    recv([logit_copy])
    logits = (logit_send[...] + logit_recv[...])[:, 0:EXPERTS]
    picked0 = jnp.sum(jnp.where(pick0, logits, 0.0), axis=1, keepdims=True)
    picked1 = jnp.sum(jnp.where(pick1, logits, 0.0), axis=1, keepdims=True)
    gate0, gate1 = jax.nn.sigmoid(picked0 - picked1), jax.nn.sigmoid(picked1 - picked0)
    places = iota((TOK, SLOTS), 1).astype(F32)
    gates = jnp.where(places == from0, gate0, 0.0) + jnp.where(places == from1, gate1, 0.0)
    gates_high = gates.astype(BF16)
    gates_low = (gates - gates_high.astype(F32)).astype(BF16)

    out_copies = []
    for ch in range(CHUNKS):
        recv(rz_copies[ch])
        moe_out = dot(gates_high, rz_recv[ch]) + dot(gates_low, rz_recv[ch])
        out_send[ch] = (after[:, ch * CW : (ch + 1) * CW] + moe_out).astype(BF16)
        out_copies.append(net.send(out_send.at[ch], out_recv.at[ch], partner))
        out_ref[:, pl.ds(pl.multiple_of(s * HALF + ch * CW, CW), CW)] = out_send[ch]
    for ch in range(CHUNKS):
        recv([out_copies[ch]])
        out_ref[:, pl.ds(pl.multiple_of((1 - s) * HALF + ch * CW, CW), CW)] = out_recv[ch]
    net.finish()


def permutations():
    i = np.arange(SLOTS)
    perm = np.zeros((SLOTS, SLOTS), np.float32)
    perm[i, i % BLOCK // CAP * BLOCK + i // BLOCK * CAP + i % CAP] = 1
    perm_kv = np.zeros((TOK, TOK), np.float32)
    for kind in range(2):
        for caption in range(2):
            for p in range(32):
                row = kind * 64 + caption * 32 + p
                perm_kv[row, p // 16 * 64 + caption * 32 + p % 16 * 2 + kind] = 1
    return jnp.asarray(perm, BF16), jnp.asarray(perm_kv, BF16)


def body(
    tokens,
    memory,
    target_len,
    source_len,
    attn_gain,
    w_query,
    w_out,
    moe_gain,
    w_router,
    expert_ids,
    w_up,
    w_down,
):
    perm, perm_kv = permutations()
    vmem = pl.BlockSpec(memory_space=pltpu.VMEM)
    smem = pl.BlockSpec(memory_space=pltpu.SMEM)
    hbm = pl.BlockSpec(memory_space=pl.ANY)
    buf = lambda *shape: pltpu.VMEM(shape, BF16)
    wide = lambda *shape: pltpu.VMEM(shape, F32)
    n_sems = 128
    return pl.pallas_call(
        kernel,
        out_shape=jax.ShapeDtypeStruct((TOK, D), BF16),
        in_specs=[vmem, vmem, smem, smem] + [vmem] * 9 + [hbm, hbm],
        out_specs=vmem,
        scratch_shapes=[
            buf(8, 8, 2, 16, HALF),
            buf(8, 8, 2, 16, HALF),
            buf(D, HALF),
            buf(HALF, D),
            buf(2, 64, HALF),
            buf(TOK, HALF),
            buf(TOK, D),
            wide(TOK, HALF),
            buf(TOK, HALF),
            buf(CHUNKS, TOK, CW),
            buf(CHUNKS, TOK, CW),
            wide(TOK, HALF),
            wide(TOK, 128),
            wide(TOK, 128),
            wide(TOK, 128),
            wide(TOK, 128),
            buf(SLOTS, TOK),
            buf(CHUNKS, SLOTS, CW),
            buf(CHUNKS, SLOTS, CW),
            buf(CHUNKS, SLOTS, CW),
            buf(2, 2, CHUNKS, SLOTS, CW),
            wide(2, SLOTS, HALF),
            buf(2, SLOTS, HALF),
            buf(2 * CHUNKS, SLOTS, CW),
            buf(2 * CHUNKS, SLOTS, CW),
            buf(2 * CHUNKS, SLOTS, CW),
            buf(CHUNKS, SLOTS, CW),
            buf(CHUNKS, SLOTS, CW),
            buf(CHUNKS, SLOTS, CW),
            buf(CHUNKS, SLOTS, CW),
            buf(CHUNKS, SLOTS, CW),
            buf(CHUNKS, SLOTS, CW),
            buf(CHUNKS, TOK, CW),
            buf(CHUNKS, TOK, CW),
            pltpu.SemaphoreType.DMA((n_sems,)),
            pltpu.SemaphoreType.DMA((n_sems,)),
            pltpu.SemaphoreType.DMA((2,)),
        ],
        compiler_params=pltpu.CompilerParams(
            collective_id=0, has_side_effects=True, vmem_limit_bytes=60 << 20
        ),
        cost_estimate=pl.CostEstimate(
            flops=8_000_000_000, bytes_accessed=12_000_000, transcendentals=300_000
        ),
    )(
        tokens,
        memory.reshape(64, D),
        target_len,
        source_len,
        attn_gain.reshape(1, D),
        w_query,
        w_out.T,
        moe_gain.reshape(1, D),
        w_router,
        expert_ids,
        expert_ids.T,
        perm,
        perm_kv,
        w_up.reshape(D, HALF),
        w_down.reshape(HALF, D),
    )


def solution(mesh):
    return jax.shard_map(
        body,
        mesh=mesh,
        in_specs=(
            P("expert", None),
            P("expert", "section", None, None),
            P("expert"),
            P("expert"),
            P(),
            P("expert", "section"),
            P("section", "expert"),
            P(),
            P(),
            P("expert", None),
            P("expert", None, "section"),
            P("expert", "section", None),
        ),
        out_specs=P("expert", None),
        check_vma=False,
    )
```

time: 794 us -> 169 us (0.21)
  waiting for transfers between devices: 589 us -> 0 us
  Pallas kernels: 0 us -> 160 us
  blocking collectives: 106 us -> 0 us
  local copies, waits for them, and re-layouts: 34.1 us -> 6.98 us
  matrix products: 19.4 us -> 0 us
  other arithmetic: 16.7 us -> 0 us
  starting transfers between devices: 14.4 us -> 0 us
  between operations: 13.5 us -> 0.01 us
    all_gather x2 -> x0, waiting for transfers between devices: 411 us -> none  [the longest x1 212 us: body(): lax.all_gather(w_out, 'expert', axis=1, tiled=True)]
    pallas_call x0 -> x1, Pallas kernels: none -> 160 us  [body(): pl.pallas_call(kernel, out_shape=jax.ShapeDtypeStruct((TOK, D), BF16), in...]
    all_to_all x1 -> x0, blocking collectives: 106 us -> none  [body(): lax.all_to_all(outgoing, 'expert', split_axis=0, concat_axis=0, tiled=True)]
    all_to_all x2 -> x0, waiting for transfers between devices: 98.6 us -> none  [the longest x1 93.6 us: body(): lax.all_to_all(part_out, 'expert', split_axis=0, concat_axis=0, tiled=True)]
    psum x2 -> x0, waiting for transfers between devices: 77.8 us -> none  [the longest x1 39.3 us: body(): lax.psum(moe_part.astype(jnp.bfloat16), 'section').astype(jnp.float32)]
    dot_general x8 -> x0, matrix products: 19.4 us -> none  [the longest x1 5.75 us: expert_part(): jnp.dot(rows, up_block, preferred_element_type=jnp.float32)]
    all_to_all x2 -> x0, starting transfers between devices: 14.1 us -> none  [the longest x1 9.28 us: body(): lax.all_to_all(part_out, 'expert', split_axis=0, concat_axis=0, tiled=True)]
    reduce_sum x7 -> x0, other arithmetic: 12.2 us -> none  [the longest x1 5.16 us: body(): jnp.sum(returned.reshape(experts, 2, capacity, width).astype(jnp.float32)...]
  transfers between devices with their start and end apart: 6 -> 0, of which waited for: 6 -> 0; matrix products, arithmetic and copies ran while one was open for 2% -> 0% of each run, Pallas kernels for 0% -> 0%
where the time goes in v1:
time: 169 us; the launch traced here: 167 us
  Pallas kernels  160 us (95%)
  local copies, waits for them, and re-layouts  6.98 us (4%)
    pallas_call x1, Pallas kernels, body(): pl.pallas_call(kernel, out_shape=jax.ShapeDtypeStruct((TOK, D), BF16), in...  160 us
    unnamed x3, local copies, waits for them, and re-layouts  5.23 us

profile of v1, /device:TPU:1, one launch (start us, length us, event | category | flops | bytes accessed | tf_op | source)
XLA Modules:
  0.0 166.9 jit_solution(12557059778247541721)
XLA Ops:
  0.0 1.4 copy.16.ids_ref
  1.4 1.7 %reshape.15.memory_ref = bf16[64,2048]{1,0:T(8,128)(2,1)} reshape(bf16[2,16,2,2048]{3,2,1,0:T(2,128)(2,1)} %param.15) | data formatting | bytes 524288 | tf_op jit(solution)/shard_map/reshape | solution.py:555
  3.1 2.0 %copy.15.w_router_ref = bf16[2048,64]{1,0:T(8,128)(2,1)} copy(bf16[2048,64]{0,1:T(8,128)(2,1)} %param.22) | data formatting | bytes 524288 | tf_op args[8]
  5.1 159.9 %shard_map.136 = bf16[128,2048]{1,0:T(8,128)(2,1)} custom-call(bf16[128,2048]{1,0:T(8,128)(2,1)} %tokens_ref.1, bf16[64,2048]{1,0:T(8,128)(2,1)} %reshape.15.memory_ref, s32[2]{0:T(128)} %target_len_ref.1, s32[2]{0:T(128)} %source_len_ref.1, f32[1,2048]{1,0:T(1,128)} %bitcast.10, bf16[16,1024]{1,0:T(8,128)(2,1)} %w_query_ref.1, bf16[16,1024]{1,0:T(8,128)(2,1)} %bitcast.9, ...), custom_call_target="tpu_custom_call" | custom-call | flops 8000000000 | bytes 12000000 | tf_op jit(solution)/shard_map/pallas_call | solution.py:503
  165.0 1.9 %copy.18 = bf16[128,2048]{1,0:T(8,128)(2,1)} copy(bf16[128,2048]{1,0:T(8,128)(2,1)} %shard_map.136) | data formatting | bytes 1048576

commit v2 on v1

v2 whole, which is shorter than its diff:
```python
import functools

import jax
import jax.numpy as jnp
import numpy as np
from jax import lax
from jax.experimental import pallas as pl
from jax.experimental.pallas import tpu as pltpu
from jax.sharding import PartitionSpec as P

MESH = pl.DeviceIdType.MESH
F32 = jnp.float32
BF16 = jnp.bfloat16

HD = 128
D = 2048
HALF = 1024
TOK = 128
CAP = 6
EXPERTS = 64
SLOTS = EXPERTS * CAP
BLOCK = 8 * CAP
CHUNKS = 4
CW = HALF // CHUNKS
NZ, NY, NX = 8, 4, 2
Z_STEPS = (4, 3, 5, 2, 6, 1, 7)
EARLY = 4
EARLY_BACK = 8
PLANE = ((2, 1), (1, 1), (3, 1), (2, 0), (0, 1), (1, 0), (3, 0))


def coords():
    s = lax.axis_index("section")
    e = lax.axis_index("expert")
    return s, e // 16, (e // 4) % 4, (e // 2) % 2, e % 2


def device(s, z, y, x, c):
    return (s, ((z * NY + y) * NX + x) * 2 + c)


class Net:
    def __init__(self, send_sem, recv_sem):
        self.send_sem, self.recv_sem = send_sem, recv_sem
        self.count, self.waiting = 0, []

    def send(self, src, dst, target):
        k = self.count
        self.count += 1
        copy = pltpu.make_async_remote_copy(
            src_ref=src,
            dst_ref=dst,
            send_sem=self.send_sem.at[k],
            recv_sem=self.recv_sem.at[k],
            device_id=target,
            device_id_type=MESH,
        )
        copy.start()
        self.waiting.append(copy)
        return copy

    def sent(self, copies):
        for copy in copies:
            copy.wait_send()
            self.waiting = [other for other in self.waiting if other is not copy]

    def finish(self):
        self.sent(list(self.waiting))


def recv(copies):
    for copy in copies:
        copy.wait_recv()


def gather_z_last(net, buf, cols, forwards):
    s, z, y, x, c = coords()
    view = lambda *idx: buf.at[(*idx, slice(None), cols)]
    sibling = device(s, z, y, x, 1 - c)
    mine = view(z, y * 2 + x, c)
    a = [net.send(mine, mine, device(s, z, (y + dy) % NY, (x + dx) % NX, c)) for dy, dx in PLANE]
    yield
    recv(a)
    slab = view(z, slice(None), c)
    up, down = device(s, (z + 1) % NZ, y, x, c), device(s, (z + 7) % NZ, y, x, c)
    u, d = net.send(slab, slab, up), net.send(slab, slab, down)
    forwards.append(net.send(slab, slab, sibling))
    for step in range(1, 4):
        yield
        recv([u])
        block = view((z + 8 - step) % NZ, slice(None), c)
        part = block if step < 3 else view((z + 8 - step) % NZ, pl.ds(0, 4), c)
        u = net.send(part, part, up)
        forwards.append(net.send(block, block, sibling))
        recv([d])
        block = view((z + step) % NZ, slice(None), c)
        part = block if step < 3 else view((z + step) % NZ, pl.ds(4, 4), c)
        d = net.send(part, part, down)
        forwards.append(net.send(block, block, sibling))
    yield
    recv([u, d])
    block = view((z + 4) % NZ, slice(None), c)
    forwards.append(net.send(block, block, sibling))
    yield


def gather_y_last(net, buf, cols, forwards):
    s, z, y, x, c = coords()
    view = lambda *idx: buf.at[(*idx, slice(None), cols)]
    sibling = device(s, z, y, x, 1 - c)
    mine = view(z, y * 2 + x, c)
    a = [net.send(mine, mine, device(s, (z + d) % NZ, y, x, c)) for d in Z_STEPS]
    yield
    recv(a)
    line = view(slice(None), y * 2 + x, c)
    b = net.send(line, line, device(s, z, y, 1 - x, c))
    yield
    recv([b])
    up, down = device(s, z, (y + 1) % NY, x, c), device(s, z, (y + 3) % NY, x, c)
    slab = view(slice(None), pl.ds(y * 2, 2), c)
    u, d = net.send(slab, slab, up), net.send(slab, slab, down)
    forwards.append(net.send(slab, slab, sibling))
    yield
    recv([u])
    below = ((y + 3) % NY) * 2
    part = view(pl.ds(0, 4), pl.ds(below, 2), c)
    u = net.send(part, part, up)
    block = view(slice(None), pl.ds(below, 2), c)
    forwards.append(net.send(block, block, sibling))
    recv([d])
    above = ((y + 1) % NY) * 2
    part = view(pl.ds(4, 4), pl.ds(above, 2), c)
    d = net.send(part, part, down)
    block = view(slice(None), pl.ds(above, 2), c)
    forwards.append(net.send(block, block, sibling))
    yield
    recv([u, d])
    block = view(slice(None), pl.ds(((y + 2) % NY) * 2, 2), c)
    forwards.append(net.send(block, block, sibling))
    yield


def iota(shape, dim):
    return lax.broadcasted_iota(jnp.int32, shape, dim)


def nt_dot(a, b):
    return lax.dot_general(a, b, (((1,), (1,)), ((), ())), preferred_element_type=F32)


def dot(a, b):
    return jnp.dot(a, b, preferred_element_type=F32)


def kernel(
    tokens_hbm,
    memory_hbm,
    target_len_ref,
    source_len_ref,
    attn_gain_ref,
    w_query_hbm,
    w_out_hbm,
    moe_gain_ref,
    w_router_hbm,
    ids_t_ref,
    perm_kv_ref,
    w_up_hbm,
    w_down_hbm,
    out_ref,
    tokens_ref,
    w_router_ref,
    wq,
    wo,
    w_up,
    w_down,
    mem,
    kv,
    normed,
    query_acc,
    context,
    head_send,
    head_recv,
    after,
    stat_send,
    stat_recv,
    logit_send,
    logit_recv,
    table,
    perm_ref,
    z_send,
    z_recv,
    p_send,
    rows,
    acc,
    hidden,
    part_send,
    part_recv,
    part_own,
    rp_send,
    rp_recv,
    rz_send,
    rz_recv,
    out_send,
    out_recv,
    send_sem,
    recv_sem,
    load_sem,
):
    s, z, y, x, c = coords()
    chip = y * 2 + x
    sibling, partner = device(s, z, y, x, 1 - c), device(1 - s, z, y, x, c)
    z_peers = [device(s, (z + d) % NZ, y, x, c) for d in Z_STEPS]
    p_peers, p_chips, p_sections = [], [], []
    for ds in (1, 0):
        for dy, dx in ((0, 0), *PLANE):
            if ds or dy or dx:
                to_s, to_y, to_x = (s + ds) % 2, (y + dy) % NY, (x + dx) % NX
                p_peers.append(device(to_s, z, to_y, to_x, c))
                p_chips.append(to_y * 2 + to_x)
                p_sections.append(to_s)

    col0 = pl.multiple_of(s * HALF, HALF)
    col1 = pl.multiple_of((1 - s) * HALF, HALF)
    load_up = pltpu.make_async_copy(w_up_hbm, w_up, load_sem.at[0])
    load_down = pltpu.make_async_copy(w_down_hbm, w_down, load_sem.at[1])
    load_mem = pltpu.make_async_copy(
        memory_hbm.at[:, :, :, pl.ds(col0, HALF)], mem.at[s], load_sem.at[2]
    )
    load_tokens = pltpu.make_async_copy(tokens_hbm, tokens_ref, load_sem.at[3])
    load_router = pltpu.make_async_copy(w_router_hbm, w_router_ref, load_sem.at[4])
    load_wq = pltpu.make_async_copy(w_query_hbm, wq.at[z, chip, c], load_sem.at[5])
    load_wo = pltpu.make_async_copy(w_out_hbm, wo.at[z, chip, c], load_sem.at[6])


    def columns(k, ss):
        return pl.ds(pl.multiple_of(k * 256 + ss * 128, 128), 128)

    barrier = pltpu.get_barrier_semaphore()
    peers = [sibling, *z_peers, *p_peers]
    for peer in peers:
        pl.semaphore_signal(barrier, inc=1, device_id=peer, device_id_type=MESH)
    for load in (load_wq, load_wo, load_tokens, load_mem, load_router):
        load.start()
    load_wq.wait()
    load_wo.wait()
    pl.semaphore_wait(barrier, len(peers))

    net = Net(send_sem, recv_sem)
    left, right = pl.ds(0, HALF // 2), pl.ds(HALF // 2, HALF // 2)
    qz_forwards, qy_forwards, oz_forwards, oy_forwards = [], [], [], []
    qz = gather_z_last(net, wq, left, qz_forwards)
    qy = gather_y_last(net, wq, right, qy_forwards)
    oz = gather_z_last(net, wo, left, oz_forwards)
    oy = gather_y_last(net, wo, right, oy_forwards)
    def norm():
        load_tokens.wait()
        values = tokens_ref[...].astype(F32)
        center = values - jnp.mean(values, axis=-1, keepdims=True)
        spread = jnp.mean(center * center, axis=-1, keepdims=True)
        normed[...] = (center * lax.rsqrt(spread + 1e-05) * attn_gain_ref[...]).astype(BF16)

    from0 = from1 = pick0 = pick1 = None

    def slots():
        nonlocal from0, from1, pick0, pick1
        tl0, tl1 = target_len_ref[0], target_len_ref[1]
        t = iota((1, TOK), 1)
        live = t < jnp.where(t < 64, tl0, tl1 + 64)
        i0, i1 = ids_t_ref[0:1, :], ids_t_ref[1:2, :]
        experts = iota((EXPERTS, TOK), 0)
        hit0, hit1 = (experts == i0) & live, (experts == i1) & live
        earlier = (iota((TOK, TOK), 0) < iota((TOK, TOK), 1)).astype(F32).astype(BF16)
        before = dot((hit0.astype(F32) + hit1.astype(F32)).astype(BF16), earlier)
        slot0 = jnp.sum(jnp.where(hit0, before, 0.0), axis=0, keepdims=True)
        slot1 = jnp.sum(jnp.where(hit1, before, 0.0), axis=0, keepdims=True)
        to0 = jnp.where(live, i0.astype(F32) * CAP + slot0, -1.0)
        to1 = jnp.where(live, i1.astype(F32) * CAP + slot1, -1.0)
        places = iota((SLOTS, TOK), 0).astype(F32)
        table[...] = ((places == to0) | (places == to1)).astype(F32).astype(BF16)

        t = iota((TOK, 1), 0)
        live = t < jnp.where(t < 64, tl0, tl1 + 64)
        eye = (iota((TOK, TOK), 0) == iota((TOK, TOK), 1)).astype(F32).astype(BF16)
        ids_col = nt_dot(eye, ids_t_ref[...].astype(F32).astype(BF16))
        i0, i1 = ids_col[:, 0:1], ids_col[:, 1:2]
        experts = iota((TOK, EXPERTS), 1).astype(F32)
        pick0, pick1 = experts == i0, experts == i1
        hit0, hit1 = pick0 & live, pick1 & live
        earlier = (iota((TOK, TOK), 1) < iota((TOK, TOK), 0)).astype(F32).astype(BF16)
        before = dot(earlier, (hit0.astype(F32) + hit1.astype(F32)).astype(BF16))
        slot0 = jnp.sum(jnp.where(hit0, before, 0.0), axis=1, keepdims=True)
        slot1 = jnp.sum(jnp.where(hit1, before, 0.0), axis=1, keepdims=True)
        from0 = jnp.where(live, i0 * CAP + slot0, -1.0)
        from1 = jnp.where(live, i1 * CAP + slot1, -1.0)

        i, j = iota((SLOTS, SLOTS), 0).astype(F32), iota((SLOTS, SLOTS), 1).astype(F32)
        block = jnp.floor((i + 0.5) * (1 / BLOCK))
        inner = i - block * BLOCK
        group = jnp.floor((inner + 0.5) * (1 / CAP))
        other = group * BLOCK + block * CAP + (inner - group * CAP)
        perm_ref[...] = (j == other).astype(F32).astype(BF16)

    def keys_values():
        load_mem.wait()
        recv([mem_copy])
        kv[...] = dot(perm_kv_ref[...], mem[...].reshape(TOK, HALF)).astype(BF16)

    def add_query(side):
        query_acc[:, side] = dot(normed[...], wq[:, :, :, :, side].reshape(D, HALF // 2))

    def query_z():
        recv(qz_forwards)
        add_query(slice(0, HALF // 2))

    def query_y():
        recv(qy_forwards)
        add_query(slice(HALF // 2, HALF))

    def attention():
        sl0, sl1 = source_len_ref[0], source_len_ref[1]
        q_row, k_col = iota((TOK, 64), 0), iota((TOK, 64), 1)
        visible = (k_col >= jnp.where(q_row < 64, 0, 32)) & (
            k_col < jnp.where(q_row < 64, sl0, sl1 + 32)
        )
        for h in range(HALF // HD):
            head = slice(h * HD, (h + 1) * HD)
            query = query_acc[:, head].astype(BF16)
            scores = nt_dot(query, kv[0:64, head]) * HD ** (-0.5)
            scores = jnp.where(visible, scores, -1e30)
            scores = jnp.exp(scores - jnp.max(scores, axis=-1, keepdims=True))
            weights = (scores / jnp.sum(scores, axis=-1, keepdims=True)).astype(BF16)
            context[:, head] = dot(weights, kv[64:128, head]).astype(BF16)

    head_copies = []

    def slab(n):
        k = (z + (0, 7, 1, 6, 2, 5, 3, 4)[n]) % NZ
        if n == 0:
            recv(oy_forwards)
        recv([oz_forwards[n]])
        product = nt_dot(context[...], wo[k].reshape(256, HALF))
        mine, theirs = product[:, 0:128], product[:, 128:256]
        keep = jnp.where(s == 1, theirs, mine)
        give = jnp.where(s == 1, mine, theirs)
        head_send[k] = give.astype(BF16)
        after[k] = tokens_ref[:, columns(k, s)].astype(F32) + keep
        head_copies.append(net.send(head_send.at[k], head_recv.at[k], partner))

    mem_copy = None

    def send_memory():
        nonlocal mem_copy
        mem_copy = net.send(memory_hbm.at[:, :, :, pl.ds(col1, HALF)], mem.at[s], partner)
        load_up.start()
        load_down.start()

    next(qy)
    next(qz)
    next(oy)
    norm()
    next(qz)
    next(qy)
    next(oz)
    send_memory()
    slots()
    next(qz)
    next(qy)
    next(oy)
    next(qz)
    next(oz)
    next(oy)
    keys_values()
    next(qy)
    next(qz)
    next(oz)
    next(qy)
    next(qz)
    query_y()
    next(oz)
    next(oy)
    query_z()
    next(oz)
    attention()
    next(oy)
    next(oz)
    slab(0)
    slab(1)
    slab(2)
    slab(3)
    slab(4)
    slab(5)
    slab(6)
    slab(7)
    recv(head_copies)
    for k in range(NZ):
        after[k] += head_recv[k].astype(F32)

    values = jnp.concatenate([after[k] for k in range(NZ)], axis=1)
    mean = jnp.mean(values, axis=-1, keepdims=True)
    center = values - mean
    square = jnp.sum(center * center, axis=-1, keepdims=True)
    diagonal = iota((TOK, TOK), 0) == iota((TOK, TOK), 1)
    to_row = lambda column: jnp.sum(jnp.where(diagonal, column, 0.0), axis=0, keepdims=True)
    to_column = lambda row: jnp.sum(jnp.where(diagonal, row, 0.0), axis=1, keepdims=True)
    stat_send[...] = jnp.where(iota((8, TOK), 0) == 0, to_row(mean), to_row(square))
    stat_copy = net.send(stat_send, stat_recv, partner)
    recv([stat_copy])
    mean_other, square_other = to_column(stat_recv[0:1, :]), to_column(stat_recv[1:2, :])
    gain = jnp.concatenate([moe_gain_ref[:, columns(k, s)] for k in range(NZ)], axis=1)
    gap = mean - mean_other
    spread = (square + square_other + gap * gap * (HALF / 2)) * (1.0 / D)
    mean = (mean + mean_other) * 0.5
    moe_in = (
        (values - mean) * lax.rsqrt(spread + 1e-05) * gain
    ).astype(BF16)

    own_z = pl.ds(pl.multiple_of(z * BLOCK, 16), BLOCK)
    own_chip = pl.ds(pl.multiple_of(chip * BLOCK, 16), BLOCK)
    z_blocks = [pl.ds(pl.multiple_of((z + d) % NZ * BLOCK, 16), BLOCK) for d in Z_STEPS]
    p_blocks = [pl.ds(pl.multiple_of(there * BLOCK, 16), BLOCK) for there in p_chips]

    def send_z(ch, source, into):
        into[ch, own_z] = source[ch, own_z]
        return [
            net.send(source.at[ch, block], into.at[ch, own_z], peer)
            for block, peer in zip(z_blocks, z_peers)
        ]

    def start_z(ch):
        z_send[ch] = dot(table[...], moe_in[:, ch * CW : (ch + 1) * CW]).astype(BF16)
        return send_z(ch, z_send, z_recv)

    def add_up(cc, ch):
        pieces = [rows[cc, ch, ss, :, k * 128 : (k + 1) * 128] for k in range(2) for ss in range(2)]
        joined = jnp.concatenate(pieces, axis=1)
        for n in range(HALF // 256):
            tile = slice(n * 256, (n + 1) * 256)
            product = dot(joined, w_up[ch * 512 : (ch + 1) * 512, tile])
            if ch == 0:
                acc[cc, :, tile] = product
            else:
                acc[cc, :, tile] += product

    def finish_up(cc):
        hidden[cc] = jnp.maximum(acc[cc], 0.0).astype(BF16)

    load_up.wait()
    load_router.wait()
    z_copies, p_copies, own_forwards = [start_z(0)], [], []

    logit_send[...] = jnp.zeros_like(logit_send)
    logit_send[:, 0:EXPERTS] = nt_dot(
        moe_in, jnp.concatenate([w_router_ref[:, columns(k, s)] for k in range(NZ)], axis=1)
    )
    logit_copy = net.send(logit_send, logit_recv, partner)

    def arrived(ch):
        recv(p_copies[ch])
        mine = rows.at[c, ch]
        own_forwards.append(net.send(mine, mine, sibling))
        add_up(c, ch)

    for ch in range(CHUNKS):
        if ch + 1 < CHUNKS:
            net.sent(z_copies[ch][:EARLY])
            z_copies.append(start_z(ch + 1))
        recv(z_copies[ch])
        p_send[ch] = dot(perm_ref[...], z_recv[ch]).astype(BF16)
        rows[c, ch, s, own_chip] = p_send[ch, own_chip]
        p_copies.append(
            [
                net.send(p_send.at[ch, block], rows.at[c, ch, s, own_chip], peer)
                for block, peer in zip(p_blocks, p_peers)
            ]
        )
        if ch == CHUNKS - 1:
            arrived(1)
            recv([own_forwards[0]])
            add_up(1 - c, 0)
        elif ch == 2:
            arrived(0)
    arrived(2)
    for ch in (1, 2):
        recv([own_forwards[ch]])
        add_up(1 - c, ch)
    arrived(3)
    finish_up(c)
    recv([own_forwards[3]])
    add_up(1 - c, 3)
    finish_up(1 - c)

    load_down.wait()

    def down(cc, ch, into):
        for k in range(2):
            tile = pl.ds(ch * 512 + k * 256, 256)
            product = dot(hidden[cc], w_down[:, tile]).astype(BF16)
            into[ch, 0, :, k * 128 : (k + 1) * 128] = product[:, 0:128]
            into[ch, 1, :, k * 128 : (k + 1) * 128] = product[:, 128:256]

    def start_part(ch):
        down(1 - c, ch, part_send)
        part_copies.append(net.send(part_send.at[ch], part_recv.at[ch], sibling))

    def start_back(ch):
        recv([part_copies[ch]])
        rp_send[ch] = (part_own[ch].astype(F32) + part_recv[ch].astype(F32)).astype(BF16)
        rp_recv[ch, s, own_chip] = rp_send[ch, s, own_chip]
        return [
            net.send(rp_send.at[ch, to_s, block], rp_recv.at[ch, s, own_chip], peer)
            for to_s, block, peer in zip(p_sections, p_blocks, p_peers)
        ]

    part_copies, rp_copies, rz_copies = [], [], []
    start_part(0)
    down(c, 0, part_own)
    start_part(1)
    rp_copies.append(start_back(0))
    down(c, 1, part_own)
    start_part(2)
    down(c, 2, part_own)
    start_part(3)
    down(c, 3, part_own)

    for ch in range(CHUNKS):
        if ch + 1 < CHUNKS:
            net.sent(rp_copies[ch][:EARLY_BACK])
            rp_copies.append(start_back(ch + 1))
        recv(rp_copies[ch])
        both = dot(perm_ref[...], rp_recv[ch, 0]) + dot(perm_ref[...], rp_recv[ch, 1])
        rz_send[ch] = both.astype(BF16)
        rz_copies.append(send_z(ch, rz_send, rz_recv))

    recv([logit_copy])
    logits = (logit_send[...] + logit_recv[...])[:, 0:EXPERTS]
    picked0 = jnp.sum(jnp.where(pick0, logits, 0.0), axis=1, keepdims=True)
    picked1 = jnp.sum(jnp.where(pick1, logits, 0.0), axis=1, keepdims=True)
    gate0, gate1 = jax.nn.sigmoid(picked0 - picked1), jax.nn.sigmoid(picked1 - picked0)
    places = iota((TOK, SLOTS), 1).astype(F32)
    gates = jnp.where(places == from0, gate0, 0.0) + jnp.where(places == from1, gate1, 0.0)
    gates_high = gates.astype(BF16)
    gates_low = (gates - gates_high.astype(F32)).astype(BF16)

    out_copies = []
    for ch in range(CHUNKS):
        recv(rz_copies[ch])
        moe_out = dot(gates_high, rz_recv[ch]) + dot(gates_low, rz_recv[ch])
        kept = jnp.concatenate([after[2 * ch], after[2 * ch + 1]], axis=1)
        out_send[ch] = (kept + moe_out).astype(BF16)
        out_copies.append(net.send(out_send.at[ch], out_recv.at[ch], partner))
        for k in range(2):
            out_ref[:, columns(2 * ch + k, s)] = out_send[ch, :, k * 128 : (k + 1) * 128]
    for ch in range(CHUNKS):
        recv([out_copies[ch]])
        for k in range(2):
            out_ref[:, columns(2 * ch + k, 1 - s)] = out_recv[ch, :, k * 128 : (k + 1) * 128]
    net.finish()


def permutation_kv():
    perm_kv = np.zeros((TOK, TOK), np.float32)
    for kind in range(2):
        for caption in range(2):
            for p in range(32):
                row = kind * 64 + caption * 32 + p
                perm_kv[row, p // 16 * 64 + caption * 32 + p % 16 * 2 + kind] = 1
    return jnp.asarray(perm_kv, BF16)


def body(
    tokens,
    memory,
    target_len,
    source_len,
    attn_gain,
    w_query,
    w_out,
    moe_gain,
    w_router,
    expert_ids,
    w_up,
    w_down,
):
    perm_kv = permutation_kv()
    vmem = pl.BlockSpec(memory_space=pltpu.VMEM)
    smem = pl.BlockSpec(memory_space=pltpu.SMEM)
    hbm = pl.BlockSpec(memory_space=pl.ANY)
    buf = lambda *shape: pltpu.VMEM(shape, BF16)
    wide = lambda *shape: pltpu.VMEM(shape, F32)
    n_sems = 320
    return pl.pallas_call(
        kernel,
        out_shape=jax.ShapeDtypeStruct((TOK, D), BF16),
        in_specs=[hbm, hbm, smem, smem, vmem, hbm, hbm, vmem, hbm, vmem, vmem, hbm, hbm],
        out_specs=vmem,
        scratch_shapes=[
            buf(TOK, D),
            buf(EXPERTS, D),
            buf(8, 8, 2, 16, HALF),
            buf(8, 8, 2, 16, HALF),
            buf(D, HALF),
            buf(HALF, D),
            buf(2, 2, 16, 2, HALF),
            buf(TOK, HALF),
            buf(TOK, D),
            wide(TOK, HALF),
            buf(TOK, HALF),
            buf(NZ, TOK, 128),
            buf(NZ, TOK, 128),
            wide(NZ, TOK, 128),
            wide(8, TOK),
            wide(8, TOK),
            wide(TOK, 128),
            wide(TOK, 128),
            buf(SLOTS, TOK),
            buf(SLOTS, SLOTS),
            buf(CHUNKS, SLOTS, CW),
            buf(CHUNKS, SLOTS, CW),
            buf(CHUNKS, SLOTS, CW),
            buf(2, CHUNKS, 2, SLOTS, CW),
            wide(2, SLOTS, HALF),
            buf(2, SLOTS, HALF),
            buf(CHUNKS, 2, SLOTS, CW),
            buf(CHUNKS, 2, SLOTS, CW),
            buf(CHUNKS, 2, SLOTS, CW),
            buf(CHUNKS, 2, SLOTS, CW),
            buf(CHUNKS, 2, SLOTS, CW),
            buf(CHUNKS, SLOTS, CW),
            buf(CHUNKS, SLOTS, CW),
            buf(CHUNKS, TOK, CW),
            buf(CHUNKS, TOK, CW),
            pltpu.SemaphoreType.DMA((n_sems,)),
            pltpu.SemaphoreType.DMA((n_sems,)),
            pltpu.SemaphoreType.DMA((7,)),
        ],
        compiler_params=pltpu.CompilerParams(
            collective_id=0, has_side_effects=True, vmem_limit_bytes=60 << 20
        ),
        cost_estimate=pl.CostEstimate(
            flops=8_000_000_000, bytes_accessed=12_000_000, transcendentals=300_000
        ),
    )(
        tokens,
        memory,
        target_len,
        source_len,
        attn_gain.reshape(1, D),
        w_query,
        w_out.T,
        moe_gain.reshape(1, D),
        w_router.T,
        expert_ids.T,
        perm_kv,
        w_up.reshape(D, HALF),
        w_down.reshape(HALF, D),
    )


def solution(mesh):
    return jax.shard_map(
        body,
        mesh=mesh,
        in_specs=(
            P("expert", None),
            P("expert", "section", None, None),
            P("expert"),
            P("expert"),
            P(),
            P("expert", "section"),
            P("section", "expert"),
            P(),
            P(),
            P("expert", None),
            P("expert", None, "section"),
            P("expert", "section", None),
        ),
        out_specs=P("expert", None),
        check_vma=False,
    )
```

time: 169 us -> 131 us (0.78)
  Pallas kernels: 160 us -> 128 us
  local copies, waits for them, and re-layouts: 6.98 us -> 1.88 us
    pallas_call x1, Pallas kernels: 160 us -> 128 us  [body(): pl.pallas_call(kernel, out_shape=jax.ShapeDtypeStruct((TOK, D), BF16), in...]
    unnamed x3 -> x1, local copies, waits for them, and re-layouts: 5.23 us -> 1.88 us
    reshape x1 -> x0, local copies, waits for them, and re-layouts: 1.75 us -> none  [body(): memory.reshape(64, D)]
where the time goes in v2:
time: 131 us; the launch traced here: 130 us
  Pallas kernels  128 us (98%)
  local copies, waits for them, and re-layouts  1.88 us (1%)
    pallas_call x1, Pallas kernels, body(): pl.pallas_call(kernel, out_shape=jax.ShapeDtypeStruct((TOK, D), BF16), in...  128 us

profile of v2, /device:TPU:1, one launch (start us, length us, event | category | flops | bytes accessed | tf_op | source)
XLA Modules:
  0.0 129.9 jit_solution(3065054576694415279)
XLA Ops:
  0.0 128.0 %shard_map.127 = bf16[128,2048]{1,0:T(8,128)(2,1)} custom-call(bf16[128,2048]{1,0:T(8,128)(2,1)} %tokens_hbm.1, bf16[2,16,2,2048]{3,2,1,0:T(2,128)(2,1)} %memory_hbm.1, s32[2]{0:T(128)} %target_len_ref.1, s32[2]{0:T(128)} %source_len_ref.1, f32[1,2048]{1,0:T(1,128)} %bitcast.11, bf16[16,1024]{1,0:T(8,128)(2,1)} %w_query_hbm.1, bf16[16,1024]{1,0:T(8,128)(2,1)} %bitcast.10, ...), custom_call_target="tpu_custom_call" | custom-call | flops 8000000000 | bytes 12000000 | tf_op jit(solution)/shard_map/pallas_call | solution.py:591
  128.0 1.9 %copy.15 = bf16[128,2048]{1,0:T(8,128)(2,1)} copy(bf16[128,2048]{1,0:T(8,128)(2,1)} %shard_map.127) | data formatting | bytes 1048576

commit v3 on v2

v3 whole, which is shorter than its diff:
```python
import math

import jax
import jax.numpy as jnp
import numpy as np
from jax import lax
from jax.experimental import pallas as pl
from jax.experimental.pallas import tpu as pltpu
from jax.sharding import PartitionSpec as P

MESH = pl.DeviceIdType.MESH
F32 = jnp.float32
BF16 = jnp.bfloat16

HD = 128
D = 2048
HALF = 1024
TOK = 128
CAP = 6
EXPERTS = 64
SLOTS = EXPERTS * CAP
BLOCK = 8 * CAP
NZ, NY, NX = 8, 4, 2
O_LEFT = 384
SENDS, RECVS = 23, 79
Z_STEPS = (4, 3, 5, 2, 6, 1, 7)
DISPATCH = ((0, 1), (1, 1), (2, 2), (4, 2), (6, 1), (7, 1))
RETURN = ((0, 1), (1, 2), (3, 2), (5, 1), (6, 1), (7, 1))
PLANE = ((2, 1), (1, 1), (3, 1), (2, 0), (0, 1), (1, 0), (3, 0))


def coords():
    s = lax.axis_index("section")
    e = lax.axis_index("expert")
    return s, e // 16, (e // 4) % 4, (e // 2) % 2, e % 2


def device(s, z, y, x, c):
    return (s, ((z * NY + y) * NX + x) * 2 + c)


class Net:
    def __init__(self, send_sem, recv_sem):
        self.send_sem, self.recv_sem = send_sem, recv_sem
        self.going, self.coming = {}, {}

    def send(self, src, dst, target, out, into):
        for groups, name in ((self.going, out), (self.coming, into)):
            groups.setdefault(name, [len(groups), 0])
            groups[name][1] += math.prod(src.shape)
        pltpu.make_async_remote_copy(
            src_ref=src,
            dst_ref=dst,
            send_sem=self.send_sem.at[self.going[out][0]],
            recv_sem=self.recv_sem.at[self.coming[into][0]],
            device_id=target,
            device_id_type=MESH,
        ).start()

    def recv(self, name, like):
        k, size = self.coming[name]
        assert size == math.prod(like.shape), name
        pltpu.make_async_copy(like, like, self.recv_sem.at[k]).wait()

    def sent(self, name, like):
        k, size = self.going[name]
        assert size == math.prod(like.shape), name
        pltpu.make_async_copy(like, like, self.send_sem.at[k]).wait()


def gather_z_last(net, buf, cols, name, groups):
    s, z, y, x, c = coords()
    view = lambda *idx: buf.at[(*idx, slice(None), cols)]
    sibling = device(s, z, y, x, 1 - c)
    up, down = device(s, (z + 1) % NZ, y, x, c), device(s, (z + 7) % NZ, y, x, c)

    def forward(n, k):
        block = view(k % NZ, slice(None), c)
        net.send(block, block, sibling, name + "f", name + "f" + groups[n])

    mine = view(z, y * 2 + x, c)
    for dy, dx in PLANE:
        net.send(mine, mine, device(s, z, (y + dy) % NY, (x + dx) % NX, c), name + "p", name + "p")
    yield
    net.recv(name + "p", view(z, pl.ds(0, 7), c))
    slab = view(z, slice(None), c)
    net.send(slab, slab, up, name, name + "u0")
    net.send(slab, slab, down, name, name + "d0")
    forward(0, z)
    for step in range(1, 4):
        yield
        for way, to, k, half in (("u", up, z + 8 - step, 0), ("d", down, z + step, 4)):
            block = view(k % NZ, slice(None), c)
            net.recv(f"{name}{way}{step - 1}", block)
            part = block if step < 3 else view(k % NZ, pl.ds(half, 4), c)
            net.send(part, part, to, name, f"{name}{way}{step}")
            forward(2 * step - (way == "u"), k)
    yield
    net.recv(name + "u3", view(0, pl.ds(0, 4), c))
    net.recv(name + "d3", view(0, pl.ds(0, 4), c))
    forward(7, z + 4)
    yield


def gather_y_last(net, buf, cols, name):
    s, z, y, x, c = coords()
    view = lambda *idx: buf.at[(*idx, slice(None), cols)]
    sibling = device(s, z, y, x, 1 - c)
    up, down = device(s, z, (y + 1) % NY, x, c), device(s, z, (y + 3) % NY, x, c)
    line = lambda dy, xx, zs=slice(None): view(zs, (y + dy) % NY * 2 + xx, c)

    def forward(dy, xx):
        net.send(line(dy, xx), line(dy, xx), sibling, name + "f", name + "f")

    def first(xx, which):
        for to in (up, down):
            net.send(line(0, xx), line(0, xx), to, name, name + which)
        forward(0, xx)

    def second(xx, which):
        net.recv(name + which, view(slice(None), pl.ds(0, 2), c))
        below, above = line(3, xx, pl.ds(0, 4)), line(1, xx, pl.ds(4, 4))
        net.send(below, below, up, name, name + which + "h")
        net.send(above, above, down, name, name + which + "h")
        forward(3, xx)
        forward(1, xx)

    def last(xx, which):
        net.recv(name + which + "h", view(slice(None), 0, c))
        forward(2, xx)

    mine = view(z, y * 2 + x, c)
    for d in Z_STEPS:
        net.send(mine, mine, device(s, (z + d) % NZ, y, x, c), name + "z", name + "z")
    yield
    net.recv(name + "z", view(pl.ds(0, 7), 0, c))
    first(x, "a")
    net.send(line(0, x), line(0, x), device(s, z, y, 1 - x, c), name, name + "x")
    yield
    second(x, "a")
    yield
    net.recv(name + "x", view(slice(None), 0, c))
    first(1 - x, "b")
    yield
    second(1 - x, "b")
    yield
    last(x, "a")
    yield
    last(1 - x, "b")
    yield


def iota(shape, dim):
    return lax.broadcasted_iota(jnp.int32, shape, dim)


def nt_dot(a, b):
    return lax.dot_general(a, b, (((1,), (1,)), ((), ())), preferred_element_type=F32)


def dot(a, b):
    return jnp.dot(a, b, preferred_element_type=F32)


def kernel(
    tokens_hbm,
    memory_hbm,
    target_len_ref,
    source_len_ref,
    attn_gain_ref,
    w_query_hbm,
    w_out_hbm,
    moe_gain_ref,
    w_router_hbm,
    ids_t_ref,
    perm_kv_ref,
    w_up_hbm,
    w_down_hbm,
    out_ref,
    tokens_ref,
    w_router_ref,
    wq,
    wo,
    w_up,
    w_down,
    mem,
    kv,
    normed,
    query_acc,
    context,
    head_send,
    head_recv,
    after,
    stat_send,
    stat_recv,
    logit_send,
    logit_recv,
    table,
    perm_ref,
    z_send,
    z_recv,
    p_send,
    rows,
    acc,
    hidden,
    part_send,
    part_recv,
    part_own,
    rp_send,
    rp_recv,
    rz_send,
    rz_recv,
    out_send,
    out_recv,
    send_sem,
    recv_sem,
    load_sem,
):
    s, z, y, x, c = coords()
    chip = y * 2 + x
    sibling, partner = device(s, z, y, x, 1 - c), device(1 - s, z, y, x, c)
    z_peers = [device(s, (z + d) % NZ, y, x, c) for d in Z_STEPS]
    p_peers, p_chips, p_sections = [], [], []
    for ds in (1, 0):
        for dy, dx in ((0, 0), *PLANE):
            if ds or dy or dx:
                to_s, to_y, to_x = (s + ds) % 2, (y + dy) % NY, (x + dx) % NX
                p_peers.append(device(to_s, z, to_y, to_x, c))
                p_chips.append(to_y * 2 + to_x)
                p_sections.append(to_s)

    col0 = pl.multiple_of(s * HALF, HALF)
    col1 = pl.multiple_of((1 - s) * HALF, HALF)
    load_up = pltpu.make_async_copy(w_up_hbm, w_up, load_sem.at[0])
    load_down = pltpu.make_async_copy(w_down_hbm, w_down, load_sem.at[1])
    load_mem = pltpu.make_async_copy(
        memory_hbm.at[:, :, :, pl.ds(col0, HALF)], mem.at[s], load_sem.at[2]
    )
    load_tokens = pltpu.make_async_copy(tokens_hbm, tokens_ref, load_sem.at[3])
    load_router = pltpu.make_async_copy(w_router_hbm, w_router_ref, load_sem.at[4])
    load_wq = pltpu.make_async_copy(w_query_hbm, wq.at[z, chip, c], load_sem.at[5])
    load_wo = pltpu.make_async_copy(w_out_hbm, wo.at[z, chip, c], load_sem.at[6])


    def columns(k, ss):
        return pl.ds(pl.multiple_of(k * 256 + ss * 128, 128), 128)

    barrier = pltpu.get_barrier_semaphore()
    peers = [sibling, *z_peers, *p_peers]
    for peer in peers:
        pl.semaphore_signal(barrier, inc=1, device_id=peer, device_id_type=MESH)
    for load in (load_wq, load_wo, load_tokens, load_mem, load_router):
        load.start()
    load_wq.wait()
    load_wo.wait()
    pl.semaphore_wait(barrier, len(peers))

    net = Net(send_sem, recv_sem)
    left, right = pl.ds(0, HALF // 2), pl.ds(HALF // 2, HALF // 2)
    less, more = pl.ds(0, O_LEFT), pl.ds(O_LEFT, HALF - O_LEFT)
    qz = gather_z_last(net, wq, left, "qz", [""] * NZ)
    qy = gather_y_last(net, wq, right, "qy")
    oz = gather_z_last(net, wo, less, "oz", ["0", "1", "1", "3", "3", "5", "5", "7"])
    oy = gather_y_last(net, wo, more, "oy")

    def norm():
        load_tokens.wait()
        values = tokens_ref[...].astype(F32)
        center = values - jnp.mean(values, axis=-1, keepdims=True)
        spread = jnp.mean(center * center, axis=-1, keepdims=True)
        normed[...] = (center * lax.rsqrt(spread + 1e-05) * attn_gain_ref[...]).astype(BF16)

    from0 = from1 = pick0 = pick1 = None

    def slots():
        nonlocal from0, from1, pick0, pick1
        tl0, tl1 = target_len_ref[0], target_len_ref[1]
        t = iota((1, TOK), 1)
        live = t < jnp.where(t < 64, tl0, tl1 + 64)
        i0, i1 = ids_t_ref[0:1, :], ids_t_ref[1:2, :]
        experts = iota((EXPERTS, TOK), 0)
        hit0, hit1 = (experts == i0) & live, (experts == i1) & live
        earlier = (iota((TOK, TOK), 0) < iota((TOK, TOK), 1)).astype(F32).astype(BF16)
        before = dot((hit0.astype(F32) + hit1.astype(F32)).astype(BF16), earlier)
        slot0 = jnp.sum(jnp.where(hit0, before, 0.0), axis=0, keepdims=True)
        slot1 = jnp.sum(jnp.where(hit1, before, 0.0), axis=0, keepdims=True)
        to0 = jnp.where(live, i0.astype(F32) * CAP + slot0, -1.0)
        to1 = jnp.where(live, i1.astype(F32) * CAP + slot1, -1.0)
        places = iota((SLOTS, TOK), 0).astype(F32)
        table[...] = ((places == to0) | (places == to1)).astype(F32).astype(BF16)

        t = iota((TOK, 1), 0)
        live = t < jnp.where(t < 64, tl0, tl1 + 64)
        eye = (iota((TOK, TOK), 0) == iota((TOK, TOK), 1)).astype(F32).astype(BF16)
        ids_col = nt_dot(eye, ids_t_ref[...].astype(F32).astype(BF16))
        i0, i1 = ids_col[:, 0:1], ids_col[:, 1:2]
        experts = iota((TOK, EXPERTS), 1).astype(F32)
        pick0, pick1 = experts == i0, experts == i1
        hit0, hit1 = pick0 & live, pick1 & live
        earlier = (iota((TOK, TOK), 1) < iota((TOK, TOK), 0)).astype(F32).astype(BF16)
        before = dot(earlier, (hit0.astype(F32) + hit1.astype(F32)).astype(BF16))
        slot0 = jnp.sum(jnp.where(hit0, before, 0.0), axis=1, keepdims=True)
        slot1 = jnp.sum(jnp.where(hit1, before, 0.0), axis=1, keepdims=True)
        from0 = jnp.where(live, i0 * CAP + slot0, -1.0)
        from1 = jnp.where(live, i1 * CAP + slot1, -1.0)

        i, j = iota((SLOTS, SLOTS), 0).astype(F32), iota((SLOTS, SLOTS), 1).astype(F32)
        block = jnp.floor((i + 0.5) * (1 / BLOCK))
        inner = i - block * BLOCK
        group = jnp.floor((inner + 0.5) * (1 / CAP))
        other = group * BLOCK + block * CAP + (inner - group * CAP)
        perm_ref[...] = (j == other).astype(F32).astype(BF16)

    def keys_values():
        load_mem.wait()
        net.recv("memory", mem.at[0])
        kv[...] = dot(perm_kv_ref[...], mem[...].reshape(TOK, HALF)).astype(BF16)

    def add_query(side):
        query_acc[:, side] = dot(normed[...], wq[:, :, :, :, side].reshape(D, HALF // 2))

    def query_z():
        net.recv("qzf", wq.at[:, :, 1 - c, :, left])
        add_query(slice(0, HALF // 2))

    def query_y():
        net.recv("qyf", wq.at[:, :, 1 - c, :, right])
        add_query(slice(HALF // 2, HALF))

    def attention():
        sl0, sl1 = source_len_ref[0], source_len_ref[1]
        q_row, k_col = iota((TOK, 64), 0), iota((TOK, 64), 1)
        visible = (k_col >= jnp.where(q_row < 64, 0, 32)) & (
            k_col < jnp.where(q_row < 64, sl0, sl1 + 32)
        )
        for h in range(HALF // HD):
            head = slice(h * HD, (h + 1) * HD)
            query = query_acc[:, head].astype(BF16)
            scores = nt_dot(query, kv[0:64, head]) * HD ** (-0.5)
            scores = jnp.where(visible, scores, -1e30)
            scores = jnp.exp(scores - jnp.max(scores, axis=-1, keepdims=True))
            weights = (scores / jnp.sum(scores, axis=-1, keepdims=True)).astype(BF16)
            context[:, head] = dot(weights, kv[64:128, head]).astype(BF16)

    def project(*ns):
        if 0 in ns:
            net.recv("oyf", wo.at[:, :, 1 - c, :, more])
        net.recv(f"ozf{ns[0]}", wo.at[pl.ds(0, len(ns)), :, 1 - c, :, less])
        ks = [(z + (0, 7, 1, 6, 2, 5, 3, 4)[n]) % NZ for n in ns]
        products = [nt_dot(context[...], wo[k].reshape(256, HALF)) for k in ks]
        for k, product in zip(ks, products):
            mine, theirs = product[:, 0:128], product[:, 128:256]
            head_send[k] = jnp.where(s == 1, mine, theirs).astype(BF16)
            after[k] = tokens_ref[:, columns(k, s)].astype(F32) + jnp.where(s == 1, theirs, mine)
        for k in ks:
            net.send(head_send.at[k], head_recv.at[k], partner, "head", "head")

    def send_memory():
        theirs = memory_hbm.at[:, :, :, pl.ds(col1, HALF)]
        net.send(theirs, mem.at[s], partner, "memory", "memory")
        load_up.start()
        load_down.start()

    next(qy)
    next(qz)
    next(oy)
    next(oz)
    norm()
    next(qz)
    next(qy)
    slots()
    next(oy)
    next(qz)
    next(oz)
    next(qy)
    next(qy)
    next(oy)
    next(oy)
    send_memory()
    next(qz)
    next(oz)
    next(qy)
    next(qy)
    next(qz)
    next(qy)
    next(oy)
    next(oy)
    next(oz)
    next(qz)
    keys_values()
    query_y()
    query_z()
    attention()
    next(oz)
    next(oy)
    project(0)
    project(1, 2)
    project(3, 4)
    project(5, 6)
    next(oz)
    project(7)
    net.recv("head", head_recv)
    for k in range(NZ):
        after[k] += head_recv[k].astype(F32)

    values = jnp.concatenate([after[k] for k in range(NZ)], axis=1)
    mean = jnp.mean(values, axis=-1, keepdims=True)
    center = values - mean
    square = jnp.sum(center * center, axis=-1, keepdims=True)
    diagonal = iota((TOK, TOK), 0) == iota((TOK, TOK), 1)
    to_row = lambda column: jnp.sum(jnp.where(diagonal, column, 0.0), axis=0, keepdims=True)
    to_column = lambda row: jnp.sum(jnp.where(diagonal, row, 0.0), axis=1, keepdims=True)
    stat_send[...] = jnp.where(iota((8, TOK), 0) == 0, to_row(mean), to_row(square))
    net.send(stat_send, stat_recv, partner, "stat", "stat")
    net.recv("stat", stat_recv)
    mean_other, square_other = to_column(stat_recv[0:1, :]), to_column(stat_recv[1:2, :])
    gain = jnp.concatenate([moe_gain_ref[:, columns(k, s)] for k in range(NZ)], axis=1)
    gap = mean - mean_other
    spread = (square + square_other + gap * gap * (HALF / 2)) * (1.0 / D)
    mean = (mean + mean_other) * 0.5
    moe_in = (
        (values - mean) * lax.rsqrt(spread + 1e-05) * gain
    ).astype(BF16)

    own_z = pl.ds(pl.multiple_of(z * BLOCK, 16), BLOCK)
    own_chip = pl.ds(pl.multiple_of(chip * BLOCK, 16), BLOCK)
    z_blocks = [pl.ds(pl.multiple_of((z + d) % NZ * BLOCK, 16), BLOCK) for d in Z_STEPS]
    p_blocks = [pl.ds(pl.multiple_of(there * BLOCK, 16), BLOCK) for there in p_chips]

    def span(chunk):
        return pl.ds(chunk[0], chunk[1])

    def slabs(chunk):
        return range(chunk[0], chunk[0] + chunk[1])

    def side_by_side(parts):
        return jnp.concatenate(list(parts), axis=1)

    def spread(into, chunk, wide):
        for n, k in enumerate(slabs(chunk)):
            into[k] = wide[:, n * 128 : (n + 1) * 128].astype(into.dtype)

    def send_z(ch, chunk, source, into, name):
        into[span(chunk), own_z] = source[span(chunk), own_z]
        for block, peer in zip(z_blocks, z_peers):
            net.send(source.at[span(chunk), block], into.at[span(chunk), own_z], peer, name, f"{name}{ch}")

    def start_z(ch):
        chunk = DISPATCH[ch]
        columns_of = slice(chunk[0] * 128, (chunk[0] + chunk[1]) * 128)
        spread(z_send, chunk, dot(table[...], moe_in[:, columns_of]))
        send_z(ch, chunk, z_send, z_recv, "z")

    def add_up(cc, chunk):
        joined = side_by_side(rows[cc, k, ss] for k in slabs(chunk) for ss in range(2))
        depth = slice(chunk[0] * 256, (chunk[0] + chunk[1]) * 256)
        for n in range(HALF // 256):
            tile = slice(n * 256, (n + 1) * 256)
            product = dot(joined, w_up[depth, tile])
            if chunk[0] == 0:
                acc[cc, :, tile] = product
            else:
                acc[cc, :, tile] += product

    def finish_up(cc):
        hidden[cc] = jnp.maximum(acc[cc], 0.0).astype(BF16)

    load_up.wait()
    load_router.wait()
    for ch in range(len(DISPATCH)):
        start_z(ch)

    logit_send[...] = jnp.zeros_like(logit_send)
    logit_send[:, 0:EXPERTS] = nt_dot(
        moe_in, jnp.concatenate([w_router_ref[:, columns(k, s)] for k in range(NZ)], axis=1)
    )
    net.send(logit_send, logit_recv, partner, "logit", "logit")

    def like_plane(chunk):
        return z_recv.at[pl.ds(0, 5), pl.ds(0, 3 * BLOCK * chunk[1])]

    def arrived(ch):
        chunk = DISPATCH[ch]
        net.recv(f"p{ch}", like_plane(chunk))
        mine = rows.at[c, span(chunk)]
        net.send(mine, mine, sibling, "f", f"f{ch}")
        add_up(c, chunk)

    def passed_on(ch):
        net.recv(f"f{ch}", rows.at[1 - c, span(DISPATCH[ch])])
        add_up(1 - c, DISPATCH[ch])

    last = len(DISPATCH) - 1
    for ch, chunk in enumerate(DISPATCH):
        net.recv(f"z{ch}", z_recv.at[span(chunk), pl.ds(0, 7 * BLOCK)])
        spread(p_send, chunk, dot(perm_ref[...], side_by_side(z_recv[k] for k in slabs(chunk))))
        rows[c, span(chunk), s, own_chip] = p_send[span(chunk), own_chip]
        for block, peer in zip(p_blocks, p_peers):
            there = rows.at[c, span(chunk), s, own_chip]
            net.send(p_send.at[span(chunk), block], there, peer, "p", f"p{ch}")
        if ch >= 2:
            arrived(ch - 2)
        if ch >= 3:
            passed_on(ch - 3)
    arrived(last - 1)
    passed_on(last - 2)
    passed_on(last - 1)
    arrived(last)
    finish_up(c)
    passed_on(last)
    finish_up(1 - c)

    load_down.wait()

    def down(cc, ch, into):
        for k in slabs(RETURN[ch]):
            product = dot(hidden[cc], w_down[:, k * 256 : (k + 1) * 256]).astype(BF16)
            into[k, 0] = product[:, 0:128]
            into[k, 1] = product[:, 128:256]

    def give_part(ch):
        where = span(RETURN[ch])
        down(1 - c, ch, part_send)
        net.send(part_send.at[where], part_recv.at[where], sibling, "part", f"part{ch}")

    def start_back(ch):
        where = span(RETURN[ch])
        net.recv(f"part{ch}", part_recv.at[where])
        rp_send[where] = (part_own[where].astype(F32) + part_recv[where].astype(F32)).astype(BF16)
        rp_recv[where, s, own_chip] = rp_send[where, s, own_chip]
        for to_s, block, peer in zip(p_sections, p_blocks, p_peers):
            there = rp_recv.at[where, s, own_chip]
            net.send(rp_send.at[where, to_s, block], there, peer, "rp", f"rp{ch}")

    give_part(0)
    down(c, 0, part_own)
    for ch in range(len(RETURN)):
        if ch + 1 < len(RETURN):
            give_part(ch + 1)
        start_back(ch)
        if ch + 1 < len(RETURN):
            down(c, ch + 1, part_own)

    for ch, chunk in enumerate(RETURN):
        net.recv(f"rp{ch}", like_plane(chunk))
        both = [dot(perm_ref[...], side_by_side(rp_recv[k, ss] for k in slabs(chunk))) for ss in range(2)]
        spread(rz_send, chunk, both[0] + both[1])
        send_z(ch, chunk, rz_send, rz_recv, "rz")

    net.recv("logit", logit_recv)
    logits = (logit_send[...] + logit_recv[...])[:, 0:EXPERTS]
    picked0 = jnp.sum(jnp.where(pick0, logits, 0.0), axis=1, keepdims=True)
    picked1 = jnp.sum(jnp.where(pick1, logits, 0.0), axis=1, keepdims=True)
    gate0, gate1 = jax.nn.sigmoid(picked0 - picked1), jax.nn.sigmoid(picked1 - picked0)
    places = iota((TOK, SLOTS), 1).astype(F32)
    gates = jnp.where(places == from0, gate0, 0.0) + jnp.where(places == from1, gate1, 0.0)
    gates_high = gates.astype(BF16)
    gates_low = (gates - gates_high.astype(F32)).astype(BF16)

    for ch, chunk in enumerate(RETURN):
        net.recv(f"rz{ch}", rz_recv.at[span(chunk), pl.ds(0, 7 * BLOCK)])
        returned = side_by_side(rz_recv[k] for k in slabs(chunk))
        moe_out = dot(gates_high, returned) + dot(gates_low, returned)
        spread(out_send, chunk, side_by_side(after[k] for k in slabs(chunk)) + moe_out)
        net.send(out_send.at[span(chunk)], out_recv.at[span(chunk)], partner, "out", "out")
        for k in slabs(chunk):
            out_ref[:, columns(k, s)] = out_send[k]
    net.recv("out", out_recv)
    for k in range(NZ):
        out_ref[:, columns(k, 1 - s)] = out_recv[k]
    like_planes = rows.at[:, pl.ds(0, 5), :, pl.ds(0, 6 * BLOCK)]
    for name, like in (
        ("memory", mem.at[0]),
        ("head", head_send),
        ("stat", stat_send),
        ("logit", logit_send),
        ("z", z_send.at[:, pl.ds(0, 7 * BLOCK)]),
        ("p", like_planes),
        ("f", rows.at[c]),
        ("part", part_send),
        ("rp", like_planes),
        ("rz", rz_send.at[:, pl.ds(0, 7 * BLOCK)]),
        ("out", out_send),
    ):
        net.sent(name, like)
    for name, buf, cols in (("qz", wq, left), ("oz", wo, less)):
        net.sent(name + "p", buf.at[0, pl.ds(0, 7), c, :, cols])
        net.sent(name, buf.at[pl.ds(0, 7), :, c, :, cols])
        net.sent(name + "f", buf.at[:, :, c, :, cols])
    for name, buf, cols in (("qy", wq, right), ("oy", wo, more)):
        net.sent(name + "z", buf.at[pl.ds(0, 7), 0, c, :, cols])
        net.sent(name, buf.at[:, pl.ds(0, 7), c, :, cols])
        net.sent(name + "f", buf.at[:, :, c, :, cols])
    assert len(net.going) <= SENDS and len(net.coming) <= RECVS, (len(net.going), len(net.coming))


def permutation_kv():
    perm_kv = np.zeros((TOK, TOK), np.float32)
    for kind in range(2):
        for caption in range(2):
            for p in range(32):
                row = kind * 64 + caption * 32 + p
                perm_kv[row, p // 16 * 64 + caption * 32 + p % 16 * 2 + kind] = 1
    return jnp.asarray(perm_kv, BF16)


def body(
    tokens,
    memory,
    target_len,
    source_len,
    attn_gain,
    w_query,
    w_out,
    moe_gain,
    w_router,
    expert_ids,
    w_up,
    w_down,
):
    perm_kv = permutation_kv()
    vmem = pl.BlockSpec(memory_space=pltpu.VMEM)
    smem = pl.BlockSpec(memory_space=pltpu.SMEM)
    hbm = pl.BlockSpec(memory_space=pl.ANY)
    buf = lambda *shape: pltpu.VMEM(shape, BF16)
    wide = lambda *shape: pltpu.VMEM(shape, F32)
    return pl.pallas_call(
        kernel,
        out_shape=jax.ShapeDtypeStruct((TOK, D), BF16),
        in_specs=[hbm, hbm, smem, smem, vmem, hbm, hbm, vmem, hbm, vmem, vmem, hbm, hbm],
        out_specs=vmem,
        scratch_shapes=[
            buf(TOK, D),
            buf(EXPERTS, D),
            buf(8, 8, 2, 16, HALF),
            buf(8, 8, 2, 16, HALF),
            buf(D, HALF),
            buf(HALF, D),
            buf(2, 2, 16, 2, HALF),
            buf(TOK, HALF),
            buf(TOK, D),
            wide(TOK, HALF),
            buf(TOK, HALF),
            buf(NZ, TOK, 128),
            buf(NZ, TOK, 128),
            wide(NZ, TOK, 128),
            wide(8, TOK),
            wide(8, TOK),
            wide(TOK, 128),
            wide(TOK, 128),
            buf(SLOTS, TOK),
            buf(SLOTS, SLOTS),
            buf(NZ, SLOTS, 128),
            buf(NZ, SLOTS, 128),
            buf(NZ, SLOTS, 128),
            buf(2, NZ, 2, SLOTS, 128),
            wide(2, SLOTS, HALF),
            buf(2, SLOTS, HALF),
            buf(NZ, 2, SLOTS, 128),
            buf(NZ, 2, SLOTS, 128),
            buf(NZ, 2, SLOTS, 128),
            buf(NZ, 2, SLOTS, 128),
            buf(NZ, 2, SLOTS, 128),
            buf(NZ, SLOTS, 128),
            buf(NZ, SLOTS, 128),
            buf(NZ, TOK, 128),
            buf(NZ, TOK, 128),
            pltpu.SemaphoreType.DMA((SENDS,)),
            pltpu.SemaphoreType.DMA((RECVS,)),
            pltpu.SemaphoreType.DMA((7,)),
        ],
        compiler_params=pltpu.CompilerParams(
            collective_id=0, has_side_effects=True, vmem_limit_bytes=60 << 20
        ),
        cost_estimate=pl.CostEstimate(
            flops=8_000_000_000, bytes_accessed=12_000_000, transcendentals=300_000
        ),
    )(
        tokens,
        memory,
        target_len,
        source_len,
        attn_gain.reshape(1, D),
        w_query,
        w_out.T,
        moe_gain.reshape(1, D),
        w_router.T,
        expert_ids.T,
        perm_kv,
        w_up.reshape(D, HALF),
        w_down.reshape(HALF, D),
    )


def solution(mesh):
    return jax.shard_map(
        body,
        mesh=mesh,
        in_specs=(
            P("expert", None),
            P("expert", "section", None, None),
            P("expert"),
            P("expert"),
            P(),
            P("expert", "section"),
            P("section", "expert"),
            P(),
            P(),
            P("expert", None),
            P("expert", None, "section"),
            P("expert", "section", None),
        ),
        out_specs=P("expert", None),
        check_vma=False,
    )
```

time: 131 us -> 120 us (0.916)
  Pallas kernels: 128 us -> 118 us
    pallas_call x1, Pallas kernels: 128 us -> 118 us  [body(): pl.pallas_call(kernel, out_shape=jax.ShapeDtypeStruct((TOK, D), BF16), in...]
where the time goes in v3:
time: 120 us
  Pallas kernels  118 us (98%)
  local copies, waits for them, and re-layouts  1.88 us (2%)
    pallas_call x1, Pallas kernels, body(): pl.pallas_call(kernel, out_shape=jax.ShapeDtypeStruct((TOK, D), BF16), in...  118 us

profile of v3, /device:TPU:1, one launch (start us, length us, event | category | flops | bytes accessed | tf_op | source)
XLA Modules:
  0.0 119.7 jit_solution(9524611428403068540)
XLA Ops:
  0.0 117.8 %shard_map.127 = bf16[128,2048]{1,0:T(8,128)(2,1)} custom-call(bf16[128,2048]{1,0:T(8,128)(2,1)} %tokens_hbm.1, bf16[2,16,2,2048]{3,2,1,0:T(2,128)(2,1)} %memory_hbm.1, s32[2]{0:T(128)} %target_len_ref.1, s32[2]{0:T(128)} %source_len_ref.1, f32[1,2048]{1,0:T(1,128)} %bitcast.11, bf16[16,1024]{1,0:T(8,128)(2,1)} %w_query_hbm.1, bf16[16,1024]{1,0:T(8,128)(2,1)} %bitcast.10, ...), custom_call_target="tpu_custom_call" | custom-call | flops 8000000000 | bytes 12000000 | tf_op jit(solution)/shard_map/pallas_call | solution.py:627
  117.8 1.9 %copy.15 = bf16[128,2048]{1,0:T(8,128)(2,1)} copy(bf16[128,2048]{1,0:T(8,128)(2,1)} %shard_map.127) | data formatting | bytes 1048576

commit v4 on v3

--- a/solution.py
+++ b/solution.py
@@ -21,11 +21,11 @@
 SLOTS = EXPERTS * CAP
 BLOCK = 8 * CAP
 NZ, NY, NX = 8, 4, 2
-O_LEFT = 384
-SENDS, RECVS = 23, 79
+O_LEFT = 512
+SENDS, RECVS = 23, 88
 Z_STEPS = (4, 3, 5, 2, 6, 1, 7)
-DISPATCH = ((0, 1), (1, 1), (2, 2), (4, 2), (6, 1), (7, 1))
-RETURN = ((0, 1), (1, 2), (3, 2), (5, 1), (6, 1), (7, 1))
+DISPATCH = ((0, 1), (1, 1), (2, 1), (3, 1), (4, 2), (6, 1), (7, 1))
+RETURN = ((0, 1), (1, 1), (2, 1), (3, 1), (4, 1), (5, 1), (6, 1), (7, 1))
 PLANE = ((2, 1), (1, 1), (3, 1), (2, 0), (0, 1), (1, 0), (3, 0))
 
 
@@ -382,17 +382,17 @@
     next(qy)
     next(qy)
     next(qz)
-    next(qy)
     next(oy)
     next(oy)
+    next(qy)
     next(oz)
     next(qz)
     keys_values()
     query_y()
+    next(oy)
     query_z()
+    next(oz)
     attention()
-    next(oz)
-    next(oy)
     project(0)
     project(1, 2)
     project(3, 4)
@@ -532,20 +532,25 @@
             there = rp_recv.at[where, s, own_chip]
             net.send(rp_send.at[where, to_s, block], there, peer, "rp", f"rp{ch}")
 
+    def back_over_z(ch):
+        chunk = RETURN[ch]
+        net.recv(f"rp{ch}", like_plane(chunk))
+        both = [dot(perm_ref[...], side_by_side(rp_recv[k, ss] for k in slabs(chunk))) for ss in range(2)]
+        spread(rz_send, chunk, both[0] + both[1])
+        send_z(ch, chunk, rz_send, rz_recv, "rz")
+
     give_part(0)
     down(c, 0, part_own)
     for ch in range(len(RETURN)):
         if ch + 1 < len(RETURN):
             give_part(ch + 1)
         start_back(ch)
+        if ch >= 3:
+            back_over_z(ch - 3)
         if ch + 1 < len(RETURN):
             down(c, ch + 1, part_own)
-
-    for ch, chunk in enumerate(RETURN):
-        net.recv(f"rp{ch}", like_plane(chunk))
-        both = [dot(perm_ref[...], side_by_side(rp_recv[k, ss] for k in slabs(chunk))) for ss in range(2)]
-        spread(rz_send, chunk, both[0] + both[1])
-        send_z(ch, chunk, rz_send, rz_recv, "rz")
+    for ch in range(len(RETURN) - 3, len(RETURN)):
+        back_over_z(ch)
 
     net.recv("logit", logit_recv)
     logits = (logit_send[...] + logit_recv[...])[:, 0:EXPERTS]

time: 120 us -> 115 us (0.958)
  Pallas kernels: 118 us -> 113 us
    pallas_call x1, Pallas kernels: 118 us -> 113 us  [body(): pl.pallas_call(kernel, out_shape=jax.ShapeDtypeStruct((TOK, D), BF16), in...]
where the time goes in v4:
time: 115 us
  Pallas kernels  113 us (98%)
  local copies, waits for them, and re-layouts  1.88 us (2%)
    pallas_call x1, Pallas kernels, body(): pl.pallas_call(kernel, out_shape=jax.ShapeDtypeStruct((TOK, D), BF16), in...  113 us

profile of v4, /device:TPU:1, one launch (start us, length us, event | category | flops | bytes accessed | tf_op | source)
XLA Modules:
  0.0 114.9 jit_solution(9756946038421631148)
XLA Ops:
  0.0 113.0 %shard_map.127 = bf16[128,2048]{1,0:T(8,128)(2,1)} custom-call(bf16[128,2048]{1,0:T(8,128)(2,1)} %tokens_hbm.1, bf16[2,16,2,2048]{3,2,1,0:T(2,128)(2,1)} %memory_hbm.1, s32[2]{0:T(128)} %target_len_ref.1, s32[2]{0:T(128)} %source_len_ref.1, f32[1,2048]{1,0:T(1,128)} %bitcast.11, bf16[16,1024]{1,0:T(8,128)(2,1)} %w_query_hbm.1, bf16[16,1024]{1,0:T(8,128)(2,1)} %bitcast.10, ...), custom_call_target="tpu_custom_call" | custom-call | flops 8000000000 | bytes 12000000 | tf_op jit(solution)/shard_map/pallas_call | solution.py:632
  113.0 1.9 %copy.15 = bf16[128,2048]{1,0:T(8,128)(2,1)} copy(bf16[128,2048]{1,0:T(8,128)(2,1)} %shard_map.127) | data formatting | bytes 1048576

commit v5 on v4

--- a/solution.py
+++ b/solution.py
@@ -22,9 +22,9 @@
 BLOCK = 8 * CAP
 NZ, NY, NX = 8, 4, 2
 O_LEFT = 512
-SENDS, RECVS = 23, 88
+SENDS, RECVS = 23, 91
 Z_STEPS = (4, 3, 5, 2, 6, 1, 7)
-DISPATCH = ((0, 1), (1, 1), (2, 1), (3, 1), (4, 2), (6, 1), (7, 1))
+DISPATCH = ((0, 1), (1, 1), (2, 1), (3, 1), (4, 1), (5, 1), (6, 1), (7, 1))
 RETURN = ((0, 1), (1, 1), (2, 1), (3, 1), (4, 1), (5, 1), (6, 1), (7, 1))
 PLANE = ((2, 1), (1, 1), (3, 1), (2, 0), (0, 1), (1, 0), (3, 0))
 
@@ -385,10 +385,10 @@
     next(oy)
     next(oy)
     next(qy)
+    keys_values()
     next(oz)
+    query_y()
     next(qz)
-    keys_values()
-    query_y()
     next(oy)
     query_z()
     next(oz)

time: 115 us -> 115 us (level)
  no operation moved by 1% of the time
where the time goes in v5:
time: 115 us; the launch traced here: 114 us
  Pallas kernels  112 us (97%)
  local copies, waits for them, and re-layouts  1.88 us (2%)
    pallas_call x1, Pallas kernels, body(): pl.pallas_call(kernel, out_shape=jax.ShapeDtypeStruct((TOK, D), BF16), in...  112 us

profile of v5, /device:TPU:1, one launch (start us, length us, event | category | flops | bytes accessed | tf_op | source)
XLA Modules:
  0.0 114.0 jit_solution(9378795767949028996)
XLA Ops:
  0.0 112.1 %shard_map.127 = bf16[128,2048]{1,0:T(8,128)(2,1)} custom-call(bf16[128,2048]{1,0:T(8,128)(2,1)} %tokens_hbm.1, bf16[2,16,2,2048]{3,2,1,0:T(2,128)(2,1)} %memory_hbm.1, s32[2]{0:T(128)} %target_len_ref.1, s32[2]{0:T(128)} %source_len_ref.1, f32[1,2048]{1,0:T(1,128)} %bitcast.11, bf16[16,1024]{1,0:T(8,128)(2,1)} %w_query_hbm.1, bf16[16,1024]{1,0:T(8,128)(2,1)} %bitcast.10, ...), custom_call_target="tpu_custom_call" | custom-call | flops 8000000000 | bytes 12000000 | tf_op jit(solution)/shard_map/pallas_call | solution.py:632
  112.2 1.9 %copy.15 = bf16[128,2048]{1,0:T(8,128)(2,1)} copy(bf16[128,2048]{1,0:T(8,128)(2,1)} %shard_map.127) | data formatting | bytes 1048576
